TPU v7x, 256 devices: a whole 4x4x8 slice. The times are simulated.
256 devices in a mesh: leaf: 8 (over z), row: 16 (over y, x), col: 2 (over core).
Axes of the slice: x: 4, y: 4, z: 8, core: 2. Of those that a mesh axis runs over, the one named last changes fastest.
Arguments:
- root_inverse: float32 [4096, 4096], P('row', ('leaf', 'col')), as said below
- panel_one: float32 [8, 4096, 2048], P('leaf', 'row', 'col'), may hold values from -0.09375 to 0.09375
- diag_one: float32 [8, 2048, 2048], P('leaf', 'row', 'col'), as said below
- panel_two: float32 [8, 1, 4096, 2048], P('leaf', None, 'row', 'col'), may hold values from -0.09375 to 0.09375
- diag_two: float32 [8, 1, 2048, 2048], P('leaf', None, 'row', 'col'), as said below
- structure: int32 [8, 1, 16], P('leaf'), may hold values from 0 to 23, as said below
Outputs:
- cross_one: float32 [8, 4096, 2048], P('leaf', 'row', 'col')
- inner_one: float32 [8, 2048, 2048], P('leaf', 'row', 'col')
- cross_root: float32 [8, 1, 4096, 2048], P('leaf', None, 'row', 'col')
- cross_sep: float32 [8, 1, 2048, 2048], P('leaf', None, 'row', 'col')
- inner_two: float32 [8, 1, 2048, 2048], P('leaf', None, 'row', 'col')
Inputs may be any that keep to these rules, and one draw needn't show every extreme that they name: `structure`: each row of the list holds 16 distinct block numbers in rising order; the first is always 0 and the last always (6144) / 256 - 1. `root_inverse`: Symmetric; diagonal entries of 1 to 3 times positive row and column scales, off-diagonal entries of size about 1 / sqrt(4096). `diag_one`: Symmetric; diagonal entries of 1 to 3 times positive row and column scales, off-diagonal entries of size about 1 / sqrt(2048). `diag_two`: Symmetric; diagonal entries of 1 to 3 times positive row and column scales, off-diagonal entries of size about 1 / sqrt(2048).
All inputs are finite; a program needn't handle non-finite values.
Results may differ from a plain program's by a relative error of at most 0.0003.
Values sent between devices are 32-bit elements; how exact they have to be, the bound alone decides.
No kernel may reach another device: no remote copies, remote signals or barrier semaphores. Data moves between devices by JAX's collectives and lax.ppermute only.
A program may use at most 192 MiB of HBM per device.

v0:
```python
import jax
import jax.numpy as jnp
from jax import lax
from jax.sharding import PartitionSpec as P

BLK = 256
LISTED = 16


def exact_dot(left, right):
    return jnp.dot(left, right, precision=lax.Precision.HIGHEST, preferred_element_type=jnp.float32)


def contract_rows(left, right):
    return lax.dot_general(
        left,
        right,
        (((0,), (0,)), ((), ())),
        precision=lax.Precision.HIGHEST,
        preferred_element_type=jnp.float32,
    )


def select_blocks(matrix, blocks, axis_pick):
    if axis_pick == 1:
        shaped = matrix.reshape(matrix.shape[0], -1, BLK)
        return jnp.take(shaped, blocks, axis=1).reshape(matrix.shape[0], LISTED * BLK)
    shaped = matrix.reshape(-1, BLK, matrix.shape[1])
    return jnp.take(shaped, blocks, axis=0).reshape(LISTED * BLK, matrix.shape[1])


def body(root_inverse, panel_one, diag_one, panel_two, diag_two, structure):
    row_count = lax.axis_size("row")
    root_rows = lax.all_gather(root_inverse, ("leaf", "col"), axis=1, tiled=True)
    upper = panel_one[0]
    panel_all = lax.all_gather(upper, "row", axis=0, tiled=True)
    cross = -exact_dot(root_rows, panel_all)
    cross_full = lax.all_gather(cross, "col", axis=1, tiled=True)
    own_inner = diag_one.shape[1]
    own_root = root_rows.shape[0]
    turned = lax.all_to_all(cross_full, "row", split_axis=1, concat_axis=0, tiled=True)
    inner = diag_one[0] - contract_rows(turned, panel_all)
    inner_full = lax.all_gather(inner, "col", axis=1, tiled=True)
    roots, seps, inners = ([], [], [])
    lower = panel_two[0, 0]
    listed = lax.all_gather(lower, "row", axis=0, tiled=True)
    blocks = structure[0, 0]
    ancestor_rows = jnp.concatenate(
        [
            jnp.concatenate([root_rows, cross_full], axis=1),
            jnp.concatenate([turned.T, inner_full], axis=1),
        ],
        axis=0,
    )
    column = -exact_dot(select_blocks(ancestor_rows, blocks, 1), listed)
    column_full = lax.all_gather(column, "col", axis=1, tiled=True)
    column_turned = lax.all_to_all(column_full, "row", split_axis=1, concat_axis=0, tiled=True)
    cols_now = column_turned.shape[1]
    grouped = column_turned.reshape(row_count, own_root + own_inner, cols_now)
    ordered = jnp.concatenate(
        [grouped[:, :own_root].reshape(-1, cols_now), grouped[:, own_root:].reshape(-1, cols_now)],
        axis=0,
    )
    inner_low = diag_two[0, 0] - contract_rows(select_blocks(ordered, blocks, 0), listed)
    roots.append(column[:own_root])
    seps.append(column[own_root:])
    inners.append(inner_low)
    return (
        cross[None],
        inner[None],
        jnp.stack(roots)[None],
        jnp.stack(seps)[None],
        jnp.stack(inners)[None],
    )


def solution(mesh):
    in_specs = (
        P("row", ("leaf", "col")),
        P("leaf", "row", "col"),
        P("leaf", "row", "col"),
        P("leaf", None, "row", "col"),
        P("leaf", None, "row", "col"),
        P("leaf", None, None),
    )
    out_specs = (
        P("leaf", "row", "col"),
        P("leaf", "row", "col"),
        P("leaf", None, "row", "col"),
        P("leaf", None, "row", "col"),
        P("leaf", None, "row", "col"),
    )
    return jax.shard_map(body, mesh=mesh, in_specs=in_specs, out_specs=out_specs, check_vma=False)
```

profile of v0, /device:TPU:225, one launch (start us, length us, event | category | flops | bytes accessed | tf_op | source)
XLA Modules:
  0.0 517.7 jit_solution(8054335007309173965)
XLA Ops:
  7.2 1.8 copy.21
  9.1 0.7 all-gather.17.cloned.1.call-update
  9.8 42.2 %all-gather.9.cloned.1.call-done = f32[256,4096]{0,1:T(8,128)} async-done(((f32[256,256]{0,1:T(8,128)}), f32[256,4096]{0,1:T(8,128)}) %all-gather.9.cloned.1.call-update) | async-done | bytes 4194320 | tf_op jit(solution)/shard_map/all_gather | solution.py:34
  52.1 118.3 %all-gather.17.cloned.1.call-done = f32[1,4096,1024]{2,1,0:T(8,128)} async-done(((f32[1,256,1024]{2,1,0:T(8,128)}), f32[1,4096,1024]{2,1,0:T(8,128)}) %all-gather.17.cloned.1.call-update) | async-done | bytes 16777232 | tf_op jit(solution)/shard_map/all_gather | solution.py:36
  170.3 18.1 %fusion.11 = f32[256,1024]{1,0:T(8,128)} fusion(f32[256,4096]{0,1:T(8,128)} %all-gather.9.cloned.1.call-done, f32[1,4096,1024]{2,1,0:T(8,128)} %all-gather.17.cloned.1.call-done), kind=kOutput, calls=%fused_computation.17 | convolution fusion | flops 12885164032 | bytes 22020096 | tf_op jit(solution)/shard_map/dot_general | solution.py:11
  188.5 16.3 %all-gather.11.cloned.1.call-done = f32[256,2048]{1,0:T(8,128)} async-done(((f32[256,1024]{1,0:T(8,128)}), f32[256,2048]{1,0:T(8,128)}) %all-gather.11.cloned.1.call-update) | async-done | bytes 2097168 | tf_op jit(solution)/shard_map/all_gather | solution.py:38
  204.7 1.8 copy_bitcast_fusion.1
  206.5 34.2 %all_to_all.35 = f32[256,16,128]{2,0,1:T(8,128)S(1)} all-to-all(f32[256,16,128]{2,0,1:T(8,128)S(1)} %copy_bitcast_fusion.1), channel_id=1, replica_groups=mesh['leaf'=8,'row'=16,'col'=2] {'row'}, dimensions={1} | all-to-all | bytes 4194304 | tf_op jit(solution)/shard_map/all_to_all | solution.py:41
  240.7 13.5 %fusion.14 = f32[128,1024]{1,0:T(8,128)} fusion(f32[4096,128]{1,0:T(8,128)S(1)} %bitcast.69, f32[1,4096,1024]{2,1,0:T(8,128)} %all-gather.17.cloned.1.call-done, f32[1,128,1024]{2,1,0:T(8,128)S(1)} %copy-done.1), kind=kOutput, calls=%fused_computation.18 | convolution fusion | flops 6442582016 | bytes 19922944 | tf_op jit(solution)/shard_map/dot_general | solution.py:15
  254.3 0.5 all-gather.19.cloned.1.call-update
  254.8 0.2 all-gather.15.cloned.1.call-start
  255.2 2.9 copy.23
  258.1 9.6 %all-gather.13.cloned.1.call-done = f32[128,2048]{1,0:T(8,128)} async-done(((f32[128,1024]{1,0:T(8,128)}), f32[128,2048]{1,0:T(8,128)}) %all-gather.13.cloned.1.call-update) | async-done | bytes 1048592 | tf_op jit(solution)/shard_map/all_gather | solution.py:43
  267.7 1.5 copy.24
  269.3 7.1 %maximum_maximum_fusion = f32[384,6144]{0,1:T(8,128)} fusion(f32[128,2048]{0,1:T(8,128)S(1)} %copy.24, f32[128,4096]{0,1:T(8,128)S(1)} %bitcast.70, f32[256,2048]{0,1:T(8,128)} %copy.23, f32[256,4096]{0,1:T(8,128)} %all-gather.9.cloned.1.call-done), kind=kLoop, calls=%fused_computation.10 | loop fusion | flops 7077888 | bytes 18874368 | tf_op jit(solution)/shard_map/concatenate | solution.py:48
  276.4 9.7 %copy.25 = f32[384,24,256]{2,0,1:T(8,128)} copy(f32[384,24,256]{0,2,1:T(8,128)} %bitcast.67) | data formatting | bytes 18874368 | tf_op jit(solution)/shard_map/reshape | solution.py:26
  286.1 7.3 %gather_fusion = f32[16,384,256]{2,1,0:T(8,128)} fusion(f32[384,24,256]{2,0,1:T(8,128)} %copy.25, s32[1024]{0:T(1024)S(1)} %pad_clamp_fusion), kind=kCustom, calls=%fused_computation | custom fusion | bytes 12582976 | tf_op jit(solution)/shard_map/jit(_take)/gather | solution.py:27
  293.4 6.6 %copy.26 = f32[384,16,256]{0,2,1:T(8,128)} copy(f32[384,16,256]{2,0,1:T(8,128)} %bitcast.68) | data formatting | bytes 12582912 | tf_op jit(solution)/shard_map/jit(_take)/gather | solution.py:27
  300.0 4.9 bitcast_select_fusion
  304.9 82.2 %all-gather.19.cloned.1.call-done = f32[1,1,4096,1024]{3,2,1,0:T(8,128)} async-done(((f32[1,1,256,1024]{3,2,1,0:T(8,128)}), f32[1,1,4096,1024]{3,2,1,0:T(8,128)}) %all-gather.19.cloned.1.call-update) | async-done | bytes 16777232 | tf_op jit(solution)/shard_map/all_gather | solution.py:46
  387.1 24.9 %fusion.8 = f32[384,1024]{1,0:T(8,128)} fusion(f32[384,4096]{0,1:T(8,128)} %bitcast_select_fusion, f32[1,1,4096,1024]{3,2,1,0:T(8,128)} %all-gather.19.cloned.1.call-done), kind=kOutput, calls=%fused_computation.16 | convolution fusion | flops 19327746048 | bytes 24641536 | tf_op jit(solution)/shard_map/dot_general | solution.py:11
  412.0 17.9 %all-gather.15.cloned.1.call-done = f32[384,2048]{1,0:T(8,128)} async-done(((f32[384,1024]{1,0:T(8,128)}), f32[384,2048]{1,0:T(8,128)}) %all-gather.15.cloned.1.call-update) | async-done | bytes 3145744 | tf_op jit(solution)/shard_map/all_gather | solution.py:56
  429.9 3.8 copy_bitcast_fusion
  433.7 6.7 %all-to-all-start.1 = ((f32[384,16,128]{2,0,1:T(8,128)}), f32[384,16,128]{2,0,1:T(8,128)}, u32[]{:S(2)}, u32[]{:S(2)}) async-start(f32[384,16,128]{2,0,1:T(8,128)} %copy_bitcast_fusion), calls=%async_computation.1 | async-start | bytes 6291456 | tf_op jit(solution)/shard_map/all_to_all | solution.py:57
  440.5 0.8 slice_bitcast_fusion.1
  441.3 1.0 slice_bitcast_fusion
  442.3 46.1 %all-to-all-done.1 = f32[384,16,128]{2,0,1:T(8,128)} async-done(((f32[384,16,128]{2,0,1:T(8,128)}), f32[384,16,128]{2,0,1:T(8,128)}, u32[]{:S(2)}, u32[]{:S(2)}) %all-to-all-start.1) | async-done | bytes 3145760 | tf_op jit(solution)/shard_map/all_to_all | solution.py:57
  488.4 1.7 slice.22
  490.2 1.3 slice.23
  491.7 2.0 gather_fusion.1
  493.7 3.7 bitcast_select_fusion.1
  497.4 13.5 %fusion.20 = f32[1,1,128,1024]{3,2,1,0:T(8,128)} fusion(f32[4096,128]{1,0:T(8,128)S(1)} %bitcast_select_fusion.1, f32[1,1,4096,1024]{3,2,1,0:T(8,128)} %all-gather.19.cloned.1.call-done, f32[1,1,128,1024]{3,2,1,0:T(8,128)S(1)} %copy-done.2), kind=kOutput, calls=%fused_computation.20 | convolution fusion | flops 6442582016 | bytes 19922944 | tf_op jit(solution)/shard_map/dot_general | solution.py:15
  (23 shorter events, 0.6 us)
Async XLA Ops:
  7.2 44.9 %all-gather.9.cloned.1.call-start = ((), (), s32[]{:S(2)}) async-start(), calls=%async_computation.2 | async-start | bytes 4456448 | tf_op jit(solution)/shard_map/all_gather | solution.py:34
  9.0 161.3 %all-gather.17.cloned.1.call-start = ((), (), s32[]{:S(2)}) async-start(), calls=%async_computation.6 | async-start | bytes 17825792 | tf_op jit(solution)/shard_map/all_gather | solution.py:36
  9.8 194.9 %all-gather.11.cloned.1.call-start = ((), (), s32[]{:S(2)}) async-start(), calls=%async_computation.3 | async-start | bytes 3145728 | tf_op jit(solution)/shard_map/all_gather | solution.py:38
  188.4 79.3 %all-gather.13.cloned.1.call-start = ((), (), s32[]{:S(2)}) async-start(), calls=%async_computation.4 | async-start | bytes 1572864 | tf_op jit(solution)/shard_map/all_gather | solution.py:43
  206.5 34.2 %copy-start.1 = (f32[1,128,1024]{2,1,0:T(8,128)S(1)}, f32[1,128,1024]{2,1,0:T(8,128)}, u32[]{:S(2)}) copy-start(f32[1,128,1024]{2,1,0:T(8,128)} %param.8) | copy-start | bytes 1572868
  240.7 14.4 %copy-start.3 = (s32[1,1,16]{2,1,0:T(1,128)S(1)}, s32[1,1,16]{2,1,0:T(1,128)}, u32[]{:S(2)}) copy-start(s32[1,1,16]{2,1,0:T(1,128)} %param.11) | copy-start | bytes 196
  254.3 132.9 %all-gather.19.cloned.1.call-start = ((), (), s32[]{:S(2)}) async-start(), calls=%async_computation.7 | async-start | bytes 17825792 | tf_op jit(solution)/shard_map/all_gather | solution.py:46
  254.8 175.0 %all-gather.15.cloned.1.call-start = ((), (), s32[]{:S(2)}) async-start(), calls=%async_computation.5 | async-start | bytes 4718592 | tf_op jit(solution)/shard_map/all_gather | solution.py:56
  433.7 6.7 %copy-start = (f32[384,1024]{1,0:T(8,128)S(1)}, f32[384,1024]{1,0:T(8,128)}, u32[]{:S(2)}) copy-start(f32[384,1024]{1,0:T(8,128)} %fusion.8) | copy-start | bytes 4718596
  433.7 54.7 %all-to-all-start.1 = ((f32[384,16,128]{2,0,1:T(8,128)}), f32[384,16,128]{2,0,1:T(8,128)}, u32[]{:S(2)}, u32[]{:S(2)}) async-start(f32[384,16,128]{2,0,1:T(8,128)} %copy_bitcast_fusion), calls=%async_computation.1 | async-start | bytes 6291456 | tf_op jit(solution)/shard_map/all_to_all | solution.py:57
  493.7 3.7 copy-start.2
Sparse Core Ops, SparseCore 0:
  10.4 41.6 all-gather.8
  54.5 115.7 all-gather.16
  188.5 16.1 all-gather.10
  254.4 13.2 all-gather.12
  270.0 117.1 all-gather.18
  412.1 17.6 all-gather.14
where the time goes:
time: 522 us; the launch traced here: 518 us
  waiting for transfers between devices  334 us (64%)
  matrix products  70 us (13%)
  local copies, waits for them, and re-layouts  42.6 us (8%)
  blocking collectives  34.2 us (7%)
  other arithmetic  15.9 us (3%)
  between operations  14.2 us (3%)
  starting transfers between devices  7.14 us (1%)
    all_gather x1, waiting for transfers between devices, body(): panel_all = lax.all_gather(upper, 'row', axis=0, tiled=True)  118 us
    all_gather x1, waiting for transfers between devices, body(): listed = lax.all_gather(lower, 'row', axis=0, tiled=True)  82.2 us
    all_to_all x1, waiting for transfers between devices, body(): lax.all_to_all(column_full, 'row', split_axis=1, concat_axis=0, tiled=True)  46.1 us
    dot_general x2, matrix products, exact_dot(): jnp.dot(left, right, precision=lax.Precision.HIGHEST, preferred_element_t...  42.9 us
    all_gather x1, waiting for transfers between devices, body(): lax.all_gather(root_inverse, ('leaf', 'col'), axis=1, tiled=True)  42.2 us
    all_to_all x1, blocking collectives, body(): lax.all_to_all(cross_full, 'row', split_axis=1, concat_axis=0, tiled=True)  34.2 us
    dot_general x2, matrix products, contract_rows(): lax.dot_general(left, right, (((0,), (0,)), ((), ())), precision=lax.Prec...  27 us
    all_gather x1, waiting for transfers between devices, body(): column_full = lax.all_gather(column, 'col', axis=1, tiled=True)  17.9 us
  transfers between devices with their start and end apart: 7, of which 7 were waited for; matrix products, arithmetic and copies ran while one was open for 8% of the time, Pallas kernels for 0%

commit v1 on v0

v1 whole, which is shorter than its diff:
```python
import functools

import jax
import jax.numpy as jnp
from jax import lax
from jax.experimental import pallas as pl
from jax.experimental.pallas import tpu as pltpu
from jax.sharding import PartitionSpec as P

BLK = 256
LANES = 128
SIDE = 4
CHIPS = SIDE * SIDE
TILE = 512
VMEM_LIMIT = 60 * 1024 * 1024
EAST, WEST, SOUTH, NORTH = (0, 1), (0, 3), (1, 0), (3, 0)


def split(value):
    high = value.astype(jnp.bfloat16)
    return high, (value - high.astype(jnp.float32)).astype(jnp.bfloat16)


def mxu(left, right):
    return jnp.dot(left, right, preferred_element_type=jnp.float32)


def three_pass(left_high, left_low, rights, widths):
    total, at = None, 0
    for ref, width in zip(rights, widths):
        for start in range(0, width, BLK):
            size = min(BLK, width - start)
            high, low = split(ref[start:start + size, :])
            ours = left_high[:, at:at + size]
            term = mxu(ours, high) + mxu(ours, low) + mxu(left_low[:, at:at + size], high)
            total = term if total is None else total + term
            at += size
    return total


def right_specs(rights):
    return [pl.BlockSpec((array.shape[0], TILE), lambda n, spots: (0, n)) for array in rights]


def call(kernel, columns, in_specs, out_specs, out_shape, scratch, flops, operands):
    return pl.pallas_call(
        kernel,
        grid_spec=pltpu.PrefetchScalarGridSpec(
            num_scalar_prefetch=1,
            grid=(columns // TILE,),
            in_specs=in_specs,
            out_specs=out_specs,
            scratch_shapes=scratch,
        ),
        out_shape=out_shape,
        compiler_params=pltpu.CompilerParams(vmem_limit_bytes=VMEM_LIMIT),
        cost_estimate=pl.CostEstimate(flops=1000, bytes_accessed=1000, transcendentals=0),
    )(*operands)


def cross_kernel(widths, has_base, spots, *refs):
    count = len(widths)
    lefts, rights, rest = refs[:count], refs[count:2 * count], refs[2 * count:]
    base = rest[0] if has_base else None
    out, left_high, left_low = rest[-3:]

    @pl.when(pl.program_id(0) == 0)
    def _():
        at = 0
        for ref, width in zip(lefts, widths):
            left_high[:, at:at + width], left_low[:, at:at + width] = split(ref[...])
            at += width

    total = three_pass(left_high, left_low, rights, widths)
    out[...] = base[...] - total if has_base else -total


def cross_sum(base, left, spots, rights):
    rows, columns = left.shape[0], rights[0].shape[1]
    widths = tuple(array.shape[0] for array in rights)
    tile = pl.BlockSpec((rows, TILE), lambda n, spots: (0, n))
    in_specs = [
        pl.BlockSpec((rows, width), functools.partial(lambda j, n, spots: (0, spots[j]), j))
        for j, width in enumerate(widths)
    ] + right_specs(rights)
    operands = [spots] + [left] * len(rights) + list(rights)
    if base is not None:
        in_specs.append(tile)
        operands.append(base)
    return call(
        functools.partial(cross_kernel, widths, base is not None),
        columns,
        in_specs,
        tile,
        jax.ShapeDtypeStruct((rows, columns), jnp.float32),
        [pltpu.VMEM((rows, sum(widths)), jnp.bfloat16)] * 2,
        6 * rows * columns * sum(widths),
        operands,
    )


def pack_kernel(core, mine, theirs, out):
    ours = pl.program_id(0) == core[0]
    for k in range(out.shape[0]):
        at = slice(k * LANES, (k + 1) * LANES)
        out[k] = jnp.where(ours, mine[:, at], theirs[:, at])


def pack(core, mine, theirs):
    rows, columns = mine.shape[0] // 2, mine.shape[1]
    half = pl.BlockSpec((rows, columns), lambda g, core: (core[0], 0))
    return pl.pallas_call(
        pack_kernel,
        grid_spec=pltpu.PrefetchScalarGridSpec(
            num_scalar_prefetch=1,
            grid=(2,),
            in_specs=[half, half],
            out_specs=pl.BlockSpec((columns // LANES, rows, LANES), lambda g, core: (g, 0, 0)),
        ),
        out_shape=jax.ShapeDtypeStruct((2 * columns // LANES, rows, LANES), jnp.float32),
        compiler_params=pltpu.CompilerParams(vmem_limit_bytes=VMEM_LIMIT),
        cost_estimate=pl.CostEstimate(flops=1000, bytes_accessed=1000, transcendentals=0),
    )(core, mine, theirs)


def in_order(is_first, mine, theirs):
    return jnp.where(is_first, mine, theirs), jnp.where(is_first, theirs, mine)


def inner_kernel(pieces, widths, listed, spots, mine, theirs, *refs):
    rights, base = refs[:len(widths)], refs[len(widths)]
    out, left_high, left_low = refs[-3:]

    @pl.when(pl.program_id(0) == 0)
    def _():
        is_first = spots[len(pieces)] == 0
        at = 0
        for j, halves in enumerate(pieces):
            spot = spots[j]
            chip = jnp.minimum(spot, CHIPS - 1)
            both = in_order(is_first, mine[chip, :LANES, :], theirs[chip, :LANES, :])
            if listed:
                first_low = jnp.clip(2 * (spot - CHIPS), 0, CHIPS - 2)
                lower = [
                    jnp.concatenate(in_order(is_first, mine[chip_low, LANES:, :], theirs[chip_low, LANES:, :]))
                    for chip_low in (first_low, first_low + 1)
                ]
                both = [jnp.where(spot < CHIPS, top, low) for top, low in zip(both, lower)]
            for half in halves:
                left_high[:, at:at + LANES], left_low[:, at:at + LANES] = split(both[half].T)
                at += LANES

    out[...] = base[...] - three_pass(left_high, left_low, rights, widths)


def inner_sum(base, mine, theirs, spots, pieces, rights, listed):
    columns = base.shape[1]
    widths = tuple(array.shape[0] for array in rights)
    whole = pl.BlockSpec(mine.shape, lambda n, spots: (0, 0, 0))
    tile = pl.BlockSpec((base.shape[0], TILE), lambda n, spots: (0, n))
    return call(
        functools.partial(inner_kernel, pieces, widths, listed),
        columns,
        [whole, whole] + right_specs(rights) + [tile],
        tile,
        jax.ShapeDtypeStruct(base.shape, jnp.float32),
        [pltpu.VMEM((base.shape[0], sum(widths)), jnp.bfloat16)] * 2,
        6 * base.shape[0] * columns * sum(widths),
        [spots, mine, theirs] + list(rights) + [base],
    )


def pick_kernel(groups, spots, root, cross_mine, cross_theirs, turned_mine, turned_theirs, mine, theirs, *outs):
    top = root.shape[0]
    count = sum(len(group) for group in groups)
    core = spots[count]
    is_first = core == 0
    j = 0
    for number, group in enumerate(groups):
        high, low = outs[2 * number], outs[2 * number + 1]
        at = 0
        for halves in group:
            spot = spots[j]
            j += 1
            for half in halves:

                def store(upper, lower, at=at):
                    high[:top, at:at + LANES], low[:top, at:at + LANES] = split(upper)
                    high[top:, at:at + LANES], low[top:, at:at + LANES] = split(lower)

                @pl.when(spot < CHIPS)
                def _():
                    columns = pl.ds(pl.multiple_of(spot * BLK + half * LANES, LANES), LANES)
                    turned = in_order(is_first, turned_mine[spot], turned_theirs[spot])[half]
                    store(root[:, columns], turned.T)

                @pl.when(spot >= CHIPS)
                def _():
                    block = spot - CHIPS
                    per_core = cross_mine.shape[1] // BLK
                    ours = block // per_core == core
                    columns = pl.ds(pl.multiple_of((block % per_core) * BLK + half * LANES, LANES), LANES)
                    store(
                        jnp.where(ours, cross_mine[:, columns], cross_theirs[:, columns]),
                        jnp.where(ours, mine[:, columns], theirs[:, columns]),
                    )

                at += LANES


def pick(spots, groups, operands):
    rows = operands[0].shape[0] + operands[-1].shape[0]
    shapes = []
    for group in groups:
        depth = LANES * sum(len(halves) for halves in group)
        shapes += [jax.ShapeDtypeStruct((rows, depth), jnp.bfloat16)] * 2
    space = pl.BlockSpec(memory_space=pltpu.VMEM)
    return pl.pallas_call(
        functools.partial(pick_kernel, groups),
        in_specs=[pl.BlockSpec(memory_space=pltpu.SMEM)] + [space] * len(operands),
        out_specs=[space] * len(shapes),
        out_shape=shapes,
        compiler_params=pltpu.CompilerParams(vmem_limit_bytes=VMEM_LIMIT),
        cost_estimate=pl.CostEstimate(flops=1000, bytes_accessed=1000, transcendentals=0),
    )(spots, *operands)


def column_kernel(widths, core, left_high, left_low, *refs):
    rights, (out_top, out_low, *turning) = refs[:len(widths)], refs[len(widths):]
    total = three_pass(left_high, left_low, rights, widths)
    top = out_top.shape[0]
    out_top[...] = -total[:top]
    out_low[...] = -total[top:]
    for ref, half in zip(turning, (core[0], 1 - core[0])):
        for k in range(TILE // LANES):
            columns = slice(k * LANES, (k + 1) * LANES)
            ref[k, :LANES] = out_top[pl.ds(pl.multiple_of(half * LANES, LANES), LANES), columns]
            ref[k, LANES:] = out_low[pl.ds(pl.multiple_of(half * (LANES // 2), LANES // 2), LANES // 2), columns]


def column_sum(core, left, rights):
    rows, depth = left[0].shape
    columns = rights[0].shape[1]
    top, low = BLK, rows - BLK
    widths = tuple(array.shape[0] for array in rights)
    whole = pl.BlockSpec((rows, depth), lambda n, core: (0, 0))
    tiles = [pl.BlockSpec((size, TILE), lambda n, core: (0, n)) for size in (top, low)]
    turning = pl.BlockSpec((TILE // LANES, rows // 2, LANES), lambda n, core: (n, 0, 0))
    shapes = [jax.ShapeDtypeStruct((size, columns), jnp.float32) for size in (top, low)]
    shapes += [jax.ShapeDtypeStruct((columns // LANES, rows // 2, LANES), jnp.float32)] * 2
    return call(
        functools.partial(column_kernel, widths),
        columns,
        [whole, whole] + right_specs(rights),
        tiles + [turning, turning],
        shapes,
        [],
        6 * rows * columns * depth,
        [core, *left, *rights],
    )


def after(value, *others):
    return lax.optimization_barrier((value,) + others)[0]


def pull(value, way):
    pairs = []
    for target in range(CHIPS):
        y, x = divmod(target, SIDE)
        pairs.append((((y + way[0]) % SIDE) * SIDE + (x + way[1]) % SIDE, target))
    return lax.ppermute(value, "row", pairs)


def other_core(value):
    return lax.ppermute(value, "col", [(0, 1), (1, 0)])


def first_round(own):
    return [pull(own, way) for way in (EAST, WEST, SOUTH, NORTH)]


def second_round(near, *gates):
    e, w, s, n = near
    es = pull(after(s, e, *gates), EAST)
    wn = pull(after(n, w, *gates), WEST)
    sw = pull(after(w, s, *gates), SOUTH)
    ne = pull(after(e, n, *gates), NORTH)
    return es, wn, sw, ne


def third_round(diagonal, *gates):
    es, wn, sw, ne = diagonal
    ees = pull(after(es, *gates), EAST)
    wwn = pull(after(wn, *gates), WEST)
    sse = pull(after(es, sw, *gates), SOUTH)
    nnw = pull(after(wn, ne, *gates), NORTH)
    return ees, wwn, sse, nnw


def fourth_round(near, third, *gates):
    e, w, s, n = near
    ees, wwn, sse, nnw = third
    half = e.shape[0] // 2
    first = pull(after(nnw[:half], wwn, *gates), WEST)
    second = pull(after(wwn[half:], nnw, *gates), NORTH)
    return pull(after(e, ees, *gates), EAST), pull(after(s, sse, *gates), SOUTH), first, second


PLACES = [
    [(0, 0), EAST, WEST, SOUTH, NORTH, (1, 1), (3, 3), (1, 3), (3, 1)],
    [(1, 2), (3, 2), (2, 1), (2, 3)],
    [(0, 2), (2, 0), (2, 2), (2, 2)],
]
WHOLE = (0, 1)
HALVES = [[WHOLE] * 9, [WHOLE] * 4, [WHOLE, WHOLE, (0,), (1,)]]


def body(root_inverse, panel_one, diag_one, panel_two, diag_two, structure):
    place = lax.axis_index("row")
    core = lax.axis_index("col").astype(jnp.int32)
    core_vector = core[None]
    blocks = structure[0, 0]
    own_upper, own_lower = panel_one[0], panel_two[0, 0]

    def chips(places):
        down = jnp.array([spot[0] for spot in places], jnp.int32)
        right = jnp.array([spot[1] for spot in places], jnp.int32)
        return ((place // SIDE + down) % SIDE) * SIDE + (place % SIDE + right) % SIDE

    halves = sum(HALVES, [])
    chip_spots = jnp.concatenate([chips(sum(PLACES, [])), core_vector])
    listed_spots = jnp.concatenate([blocks, core_vector])
    natural = [WHOLE] * blocks.shape[0]
    late_spots = chips(PLACES[1] + PLACES[2])
    scale = jnp.array([1] * 6 + [2, 2], jnp.int32)
    late_spots = late_spots * scale + jnp.array([0] * 7 + [1], jnp.int32)

    root_rows = lax.all_gather(root_inverse, ("leaf", "col"), axis=1, tiled=True)

    near = first_round(own_upper)
    diagonal = second_round(near)
    third = third_round(diagonal)
    lower = lax.all_gather(after(own_lower, *near), "row", axis=0, tiled=True)
    early = [own_upper, *near, *diagonal]
    cross = cross_sum(None, root_rows, chips(PLACES[0]), early)
    fourth = fourth_round(near, third)
    upper = [*early, *third, *fourth]
    cross = cross_sum(cross, root_rows, late_spots, [*third, *fourth])
    cross_theirs = other_core(cross)
    sent = pack(core_vector, cross, cross_theirs)
    turned = lax.all_to_all(sent, "row", split_axis=0, concat_axis=0, tiled=True)
    turned_theirs = other_core(turned)
    inner = inner_sum(diag_one[0], turned, turned_theirs, chip_spots, halves, upper, False)
    inner_theirs = other_core(inner)

    picked = pick(
        listed_spots, [natural], (root_rows, cross, cross_theirs, turned, turned_theirs, inner, inner_theirs)
    )
    top, low, keep, give = column_sum(core_vector, picked, [lower])

    theirs = other_core(give)
    sent = jnp.concatenate(in_order(core == 0, keep, theirs), axis=0)
    turned = lax.all_to_all(sent, "row", split_axis=0, concat_axis=0, tiled=True)
    inner_low = inner_sum(diag_two[0, 0], turned, other_core(turned), listed_spots, natural, [lower], True)
    return cross[None], inner[None], top[None, None], low[None, None], inner_low[None, None]


def solution(mesh):
    in_specs = (
        P("row", ("leaf", "col")),
        P("leaf", "row", "col"),
        P("leaf", "row", "col"),
        P("leaf", None, "row", "col"),
        P("leaf", None, "row", "col"),
        P("leaf", None, None),
    )
    out_specs = (
        P("leaf", "row", "col"),
        P("leaf", "row", "col"),
        P("leaf", None, "row", "col"),
        P("leaf", None, "row", "col"),
        P("leaf", None, "row", "col"),
    )
    return jax.shard_map(body, mesh=mesh, in_specs=in_specs, out_specs=out_specs, check_vma=False)
```

time: 522 us -> 293 us (0.56)
  waiting for transfers between devices: 334 us -> 101 us
  matrix products: 70 us -> 0 us
  Pallas kernels: 0 us -> 67.5 us
  local copies, waits for them, and re-layouts: 42.6 us -> 5.67 us
  starting transfers between devices: 7.14 us -> 43 us
  blocking collectives: 34.2 us -> 58 us
  other arithmetic: 15.9 us -> 3.58 us
    all_gather x5 -> x1, waiting for transfers between devices: 244 us -> 0.01 us  [body(): lower = lax.all_gather(after(own_lower, *near), 'row', axis=0, tiled=True)]
    ppermute x0 -> x21, waiting for transfers between devices: none -> 100 us  [the longest x16 89.6 us: pull(): return lax.ppermute(value, 'row', pairs)]
    dot_general x4 -> x0, matrix products: 70 us -> none  [the longest x2 42.9 us: exact_dot(): jnp.dot(left, right, precision=lax.Precision.HIGHEST, preferred_element_t...]
    pallas_call x0 -> x7, Pallas kernels: none -> 67.5 us  [the longest x5 55.6 us: call(): pl.pallas_call(kernel, grid_spec=pltpu.PrefetchScalarGridSpec(num_scalar_...]
    all_to_all x1 -> x0, waiting for transfers between devices: 46.1 us -> none  [body(): lax.all_to_all(column_full, 'row', split_axis=1, concat_axis=0, tiled=True)]
    ppermute x0 -> x21, starting transfers between devices: none -> 43 us  [the longest x5 23.1 us: other_core(): return lax.ppermute(value, 'col', [(0, 1), (1, 0)])]
    all_gather x1, waiting for transfers between devices: 42.2 us -> 0.01 us  [body(): lax.all_gather(root_inverse, ('leaf', 'col'), axis=1, tiled=True)]
    all_to_all x1 -> x2, blocking collectives: 34.2 us -> 58 us  [body(): lax.all_to_all(sent, 'row', split_axis=0, concat_axis=0, tiled=True)]
  transfers between devices with their start and end apart: 7 -> 23, of which waited for: 7 -> 15; matrix products, arithmetic and copies ran while one was open for 8% -> 1% of each run, Pallas kernels for 0% -> 14%
where the time goes in v1:
time: 293 us
  waiting for transfers between devices  101 us (34%)
  Pallas kernels  67.5 us (23%)
  blocking collectives  58 us (20%)
  starting transfers between devices  43 us (15%)
  between operations  14.3 us (5%)
  local copies, waits for them, and re-layouts  5.67 us (2%)
  other arithmetic  3.58 us (1%)
    ppermute x16, waiting for transfers between devices, pull(): return lax.ppermute(value, 'row', pairs)  89.6 us
    all_to_all x2, blocking collectives, body(): lax.all_to_all(sent, 'row', split_axis=0, concat_axis=0, tiled=True)  58 us
    pallas_call x5, Pallas kernels, call(): pl.pallas_call(kernel, grid_spec=pltpu.PrefetchScalarGridSpec(num_scalar_...  55.6 us
    ppermute x5, starting transfers between devices, other_core(): return lax.ppermute(value, 'col', [(0, 1), (1, 0)])  23.1 us
    ppermute x16, starting transfers between devices, pull(): return lax.ppermute(value, 'row', pairs)  19.9 us
    ppermute x5, waiting for transfers between devices, other_core(): return lax.ppermute(value, 'col', [(0, 1), (1, 0)])  10.5 us
    pallas_call x1, Pallas kernels, pick(): pl.pallas_call(functools.partial(pick_kernel, groups), in_specs=[pl.Block...  9.67 us
  transfers between devices with their start and end apart: 23, of which 15 were waited for; matrix products, arithmetic and copies ran while one was open for 1% of the time, Pallas kernels for 14%

profile of v1, /device:TPU:225, one launch (start us, length us, event | category | flops | bytes accessed | tf_op | source)
XLA Modules:
  0.0 292.9 jit_solution(3248844202119759227)
XLA Ops:
  7.9 2.8 collective-permute-start
  10.8 2.5 collective-permute-start.1
  13.2 19.7 %collective-permute-done.refs_12_.refs_3_ = f32[256,1024]{1,0:T(8,128)S(1)} collective-permute-done((f32[256,1024]{1,0:T(8,128)}, f32[256,1024]{1,0:T(8,128)S(1)}, u32[]{:S(2)}, u32[]{:S(2)}) %collective-permute-start) | collective-permute-done | bytes 1048608 | tf_op jit(solution)/shard_map/ppermute | solution.py:272
  32.9 2.2 collective-permute-done.1.refs_10_.refs_1_
  35.1 3.1 %collective-permute-done.4.refs_13_.refs_4_ = f32[256,1024]{1,0:T(8,128)S(1)} collective-permute-done((f32[256,1024]{1,0:T(8,128)}, f32[256,1024]{1,0:T(8,128)S(1)}, u32[]{:S(2)}, u32[]{:S(2)}) %collective-permute-start.4) | collective-permute-done | bytes 1048608 | tf_op jit(solution)/shard_map/ppermute | solution.py:272
  38.9 1.9 collective-permute-start.8
  40.8 1.4 collective-permute-start.6
  42.2 18.7 %collective-permute-done.2.refs_14_.refs_5_ = f32[256,1024]{1,0:T(8,128)S(1)} collective-permute-done((f32[256,1024]{1,0:T(8,128)S(1)}, f32[256,1024]{1,0:T(8,128)S(1)}, u32[]{:S(2)}, u32[]{:S(2)}) %collective-permute-start.2) | collective-permute-done | bytes 1048608 | tf_op jit(solution)/shard_map/ppermute | solution.py:272
  61.4 3.0 %collective-permute-start.9 = (f32[256,1024]{1,0:T(8,128)S(1)}, f32[256,1024]{1,0:T(8,128)S(1)}, u32[]{:S(2)}, u32[]{:S(2)}) collective-permute-start(f32[256,1024]{1,0:T(8,128)S(1)} %collective-permute-done.2.refs_14_.refs_5_), channel_id=1, source_target_pairs={{8,0},{10,2},{12,4},{14,6},{16,8},{18,10},{20,12},{22,14},{24,16},... | collective-permute-start | bytes 3145736 | tf_op jit(solution)/shard_map/ppermute | solution.py:272
  64.6 1.5 collective-permute-start.7
  66.1 33.5 %collective-permute-done.9.refs_10_.refs_11_ = f32[256,1024]{1,0:T(8,128)S(1)} collective-permute-done((f32[256,1024]{1,0:T(8,128)S(1)}, f32[256,1024]{1,0:T(8,128)S(1)}, u32[]{:S(2)}, u32[]{:S(2)}) %collective-permute-start.9) | collective-permute-done | bytes 1048608 | tf_op jit(solution)/shard_map/ppermute | solution.py:272
  99.6 3.5 %collective-permute-start.13 = (f32[256,1024]{1,0:T(8,128)S(1)}, f32[256,1024]{1,0:T(8,128)}, u32[]{:S(2)}, u32[]{:S(2)}) collective-permute-start(f32[256,1024]{1,0:T(8,128)S(1)} %collective-permute-done.refs_12_.refs_3_), channel_id=1, source_target_pairs={{8,0},{10,2},{12,4},{14,6},{16,8},{18,10},{20,12},{22,14},{24,16},... | collective-permute-start | bytes 3145736 | tf_op jit(solution)/shard_map/ppermute | solution.py:272
  103.6 1.3 collective-permute-start.12
  105.8 1.3 collective-permute-start.14
  109.0 9.7 %shard_map.173.refs_16_ = f32[256,1024]{1,0:T(8,128)} custom-call(s32[9]{0:T(128)} %fusion.1.spots, f32[256,4096]{1,0:T(8,128)} %all-gather.3.cloned.1.call-done.refs_0_.refs_1_.refs_2_.refs_3_.refs_4_.refs_5_.refs_6_.refs_7_.refs_8_.root, ...), custom_call_target="tpu_custom_call" | custom-call | flops 1000 | bytes 1000 | tf_op jit(solution)/shard_map/pallas_call | solution.py:46
  118.9 9.6 %collective-permute-done.13.refs_13_.refs_14_ = f32[256,1024]{1,0:T(8,128)} collective-permute-done((f32[256,1024]{1,0:T(8,128)S(1)}, f32[256,1024]{1,0:T(8,128)}, u32[]{:S(2)}, u32[]{:S(2)}) %collective-permute-start.13) | collective-permute-done | bytes 1048608 | tf_op jit(solution)/shard_map/ppermute | solution.py:272
  128.5 1.7 collective-permute-done.12.refs_12_.refs_13_
  130.2 8.8 %shard_map.174.mine.cross_mine = f32[256,1024]{1,0:T(8,128)} custom-call(s32[8]{0:T(128)} %fusion.7.spots, f32[256,4096]{1,0:T(8,128)} %all-gather.3.cloned.1.call-done.refs_0_.refs_1_.refs_2_.refs_3_.refs_4_.refs_5_.refs_6_.refs_7_.refs_8_.root, ...), custom_call_target="tpu_custom_call" | custom-call | flops 1000 | bytes 1000 | tf_op jit(solution)/shard_map/pallas_call | solution.py:46
  139.0 18.9 %collective-permute-start.16 = (f32[256,1024]{1,0:T(8,128)}, f32[256,1024]{1,0:T(8,128)S(1)}, u32[]{:S(2)}, u32[]{:S(2)}) collective-permute-start(f32[256,1024]{1,0:T(8,128)} %shard_map.174.mine.cross_mine), channel_id=1, source_target_pairs={{0,1},{1,0},{2,3},{3,2},{4,5},{5,4},{6,7},{7,6},{8,9},{9,8},{10,11... | collective-permute-start | bytes 3145736 | tf_op jit(solution)/shard_map/ppermute | solution.py:276
  157.9 2.5 collective-permute-done.16.theirs.cross_theirs
  161.3 2.3 shard_map.175
  163.6 33.0 %all_to_all.10.mine.turned_mine = f32[16,128,128]{2,1,0:T(8,128)S(1)} all-to-all(f32[16,128,128]{2,1,0:T(8,128)} %shard_map.175), channel_id=1, replica_groups=mesh['leaf'=8,'row'=16,'col'=2] {'row'}, dimensions={0} | all-to-all | bytes 2097152 | tf_op jit(solution)/shard_map/all_to_all | solution.py:352
  196.7 1.8 collective-permute-start.17
  199.1 1.7 collective-permute-done.17.theirs.turned_theirs
  201.7 10.4 %shard_map.176.mine = f32[128,1024]{1,0:T(8,128)} custom-call(s32[18]{0:T(128)} %pad_add_fusion.spots, f32[16,128,128]{2,1,0:T(8,128)} %copy-done, f32[16,128,128]{2,1,0:T(8,128)} %copy-done.13, f32[256,1024]{1,0:T(8,128)} %bitcast.17, f32[256,1024]{1,0:T(8,128)} %copy-done.5, f32[256,1024]{1,0:T(8,128)} %collective-permute-done.5.refs_11_.refs_2_, ...), custom_call_target="tpu_custom_call" | custom-call | flops 1000 | bytes 1000 | tf_op jit(solution)/shard_map/pallas_call | solution.py:46
  215.1 9.7 %shard_map.177 = (bf16[384,4096]{1,0:T(8,128)(2,1)}, bf16[384,4096]{1,0:T(8,128)(2,1)}) custom-call(s32[17]{0:T(128)} %pad_add_fusion.1.spots, f32[256,4096]{1,0:T(8,128)} %all-gather.3.cloned.1.call-done.refs_0_.refs_1_.refs_2_.refs_3_.refs_4_.refs_5_.refs_6_.refs_7_.refs_8_.root, f32[256,1024]{1,0:T(8,128)} %shard_map.174.mine.cross_mine, ...), custom_call_target="tpu_custom_call" | custom-call | flops 1000 | bytes 1000 | tf_op jit(solution)/shard_map/pallas_call | solution.py:218
  224.8 16.6 %shard_map.178 = (f32[256,1024]{1,0:T(8,128)}, f32[128,1024]{1,0:T(8,128)}, f32[8,192,128]{2,1,0:T(8,128)}, f32[8,192,128]{2,1,0:T(8,128)}) custom-call(s32[1]{0:T(128)} %bitcast.2.core, bf16[384,4096]{1,0:T(8,128)(2,1)} %get-tuple-element.32.left_high, bf16[384,4096]{1,0:T(8,128)(2,1)} %get-tuple-element.33.left_low, ...), custom_call_target="tpu_custom_call" | custom-call | flops 1000 | bytes 1000 | tf_op jit(solution)/shard_map/pallas_call | solution.py:46
  241.7 2.1 collective-permute-done.19
  245.2 24.9 %all_to_all.11.mine = f32[16,192,128]{2,1,0:T(8,128)S(1)} all-to-all(f32[16,192,128]{2,1,0:T(8,128)S(1)} %pad_maximum_fusion), channel_id=1, replica_groups=mesh['leaf'=8,'row'=16,'col'=2] {'row'}, dimensions={0} | all-to-all | bytes 3145728 | tf_op jit(solution)/shard_map/all_to_all | solution.py:364
  270.2 1.5 collective-permute-start.20
  271.7 3.0 %collective-permute-done.20.theirs = f32[16,192,128]{2,1,0:T(8,128)S(1)} collective-permute-done((f32[16,192,128]{2,1,0:T(8,128)S(1)}, f32[16,192,128]{2,1,0:T(8,128)S(1)}, u32[]{:S(2)}, u32[]{:S(2)}) %collective-permute-start.20) | collective-permute-done | bytes 1572896 | tf_op jit(solution)/shard_map/ppermute | solution.py:276
  275.9 10.2 %shard_map.179 = f32[128,1024]{1,0:T(8,128)} custom-call(s32[17]{0:T(128)} %pad_add_fusion.1.spots, f32[16,192,128]{2,1,0:T(8,128)} %copy-done.3, f32[16,192,128]{2,1,0:T(8,128)} %copy-done.15, f32[4096,1024]{1,0:T(8,128)} %all-gather.5.cloned.1.call-done.refs_0_, f32[128,1024]{1,0:T(8,128)} %bitcast.21), custom_call_target="tpu_custom_call" | custom-call | flops 1000 | bytes 1000 | tf_op jit(solution)/shard_map/pallas_call | solution.py:46
  (86 shorter events, 14.1 us)
Async XLA Ops:
  7.2 101.9 %all-gather.3.cloned.1.call-start = ((), (), s32[]{:S(2)}) async-start(), calls=%async_computation.2 | async-start | bytes 4456448 | tf_op jit(solution)/shard_map/all_gather | solution.py:339
  7.9 216.9 %all-gather.5.cloned.1.call-start = ((), (), s32[]{:S(2)}) async-start(), calls=%async_computation.3 | async-start | bytes 17825792 | tf_op jit(solution)/shard_map/all_gather | solution.py:344
  7.9 25.0 %collective-permute-start = (f32[256,1024]{1,0:T(8,128)}, f32[256,1024]{1,0:T(8,128)S(1)}, u32[]{:S(2)}, u32[]{:S(2)}) collective-permute-start(f32[256,1024]{1,0:T(8,128)} %bitcast.12), channel_id=1, source_target_pairs={{8,0},{10,2},{12,4},{14,6},{16,8},{18,10},{20,12},{22,14},{24,16},... | collective-permute-start | bytes 3145736 | tf_op jit(solution)/shard_map/ppermute | solution.py:272
  10.8 24.3 %collective-permute-start.1 = (f32[256,1024]{1,0:T(8,128)}, f32[256,1024]{1,0:T(8,128)S(1)}, u32[]{:S(2)}, u32[]{:S(2)}) collective-permute-start(f32[256,1024]{1,0:T(8,128)} %bitcast.13), channel_id=1, source_target_pairs={{2,0},{4,2},{6,4},{0,6},{10,8},{12,10},{14,12},{8,14},{18,16},{20,... | collective-permute-start | bytes 3145736 | tf_op jit(solution)/shard_map/ppermute | solution.py:272
  13.2 24.9 %collective-permute-start.4 = (f32[256,1024]{1,0:T(8,128)}, f32[256,1024]{1,0:T(8,128)S(1)}, u32[]{:S(2)}, u32[]{:S(2)}) collective-permute-start(f32[256,1024]{1,0:T(8,128)} %bitcast.14), channel_id=1, source_target_pairs={{24,0},{26,2},{28,4},{30,6},{0,8},{2,10},{4,12},{6,14},{8,16},{10,... | collective-permute-start | bytes 3145736 | tf_op jit(solution)/shard_map/ppermute | solution.py:272
  13.2 24.9 %collective-permute-start.5 = (f32[256,1024]{1,0:T(8,128)}, f32[256,1024]{1,0:T(8,128)}, u32[]{:S(2)}, u32[]{:S(2)}) collective-permute-start(f32[256,1024]{1,0:T(8,128)} %bitcast.15), channel_id=1, source_target_pairs={{6,0},{0,2},{2,4},{4,6},{14,8},{8,10},{10,12},{12,14},{22,16},{16,... | collective-permute-start | bytes 3145736 | tf_op jit(solution)/shard_map/ppermute | solution.py:272
  32.9 75.0 %copy-start.4 = (f32[256,1024]{1,0:T(8,128)}, f32[256,1024]{1,0:T(8,128)S(1)}, u32[]{:S(2)}) copy-start(f32[256,1024]{1,0:T(8,128)S(1)} %collective-permute-done.refs_12_.refs_3_) | copy-start | bytes 3145732
  38.2 69.8 %copy-start.23 = (s32[9]{0:T(128)S(1)}, s32[9]{0:T(128)}, u32[]{:S(2)}) copy-start(s32[9]{0:T(128)} %constant.107.clone) | copy-start | bytes 112
  38.2 69.8 %copy-start.24 = (s32[9]{0:T(128)S(1)}, s32[9]{0:T(128)}, u32[]{:S(2)}) copy-start(s32[9]{0:T(128)} %constant.108.clone) | copy-start | bytes 112
  38.2 70.3 %copy-start.19 = (s32[8]{0:T(128)S(1)}, s32[8]{0:T(128)}, u32[]{:S(2)}) copy-start(s32[8]{0:T(128)} %constant.103.clone) | copy-start | bytes 100
  38.2 70.3 %copy-start.20 = (s32[8]{0:T(128)S(1)}, s32[8]{0:T(128)}, u32[]{:S(2)}) copy-start(s32[8]{0:T(128)} %constant.104.clone) | copy-start | bytes 100
  38.2 70.3 %copy-start.21 = (s32[8]{0:T(128)S(1)}, s32[8]{0:T(128)}, u32[]{:S(2)}) copy-start(s32[8]{0:T(128)} %constant.105.clone) | copy-start | bytes 100
  38.2 70.3 %copy-start.22 = (s32[8]{0:T(128)S(1)}, s32[8]{0:T(128)}, u32[]{:S(2)}) copy-start(s32[8]{0:T(128)} %constant.106.clone) | copy-start | bytes 100
  38.3 22.6 %collective-permute-start.2 = (f32[256,1024]{1,0:T(8,128)S(1)}, f32[256,1024]{1,0:T(8,128)S(1)}, u32[]{:S(2)}, u32[]{:S(2)}) collective-permute-start(f32[256,1024]{1,0:T(8,128)S(1)} %collective-permute-done.refs_12_.refs_3_), channel_id=1, source_target_pairs={{2,0},{4,2},{6,4},{0,6},{10,8},{12,10},{14,12},{8,14},{18,16},{20,... | collective-permute-start | bytes 3145736 | tf_op jit(solution)/shard_map/ppermute | solution.py:272
  38.9 22.5 %collective-permute-start.8 = (f32[256,1024]{1,0:T(8,128)}, f32[256,1024]{1,0:T(8,128)S(1)}, u32[]{:S(2)}, u32[]{:S(2)}) collective-permute-start(f32[256,1024]{1,0:T(8,128)} %collective-permute-done.5.refs_11_.refs_2_), channel_id=1, source_target_pairs={{8,0},{10,2},{12,4},{14,6},{16,8},{18,10},{20,12},{22,14},{24,16},... | collective-permute-start | bytes 3145736 | tf_op jit(solution)/shard_map/ppermute | solution.py:272
  40.8 23.7 %collective-permute-start.10 = (f32[256,1024]{1,0:T(8,128)S(1)}, f32[256,1024]{1,0:T(8,128)S(1)}, u32[]{:S(2)}, u32[]{:S(2)}) collective-permute-start(f32[256,1024]{1,0:T(8,128)S(1)} %collective-permute-done.1.refs_10_.refs_1_), channel_id=1, source_target_pairs={{24,0},{26,2},{28,4},{30,6},{0,8},{2,10},{4,12},{6,14},{8,16},{10,... | collective-permute-start | bytes 3145736 | tf_op jit(solution)/shard_map/ppermute | solution.py:272
  40.8 23.7 %collective-permute-start.6 = (f32[256,1024]{1,0:T(8,128)S(1)}, f32[256,1024]{1,0:T(8,128)S(1)}, u32[]{:S(2)}, u32[]{:S(2)}) collective-permute-start(f32[256,1024]{1,0:T(8,128)S(1)} %collective-permute-done.4.refs_13_.refs_4_), channel_id=1, source_target_pairs={{6,0},{0,2},{2,4},{4,6},{14,8},{8,10},{10,12},{12,14},{22,16},{16,... | collective-permute-start | bytes 3145736 | tf_op jit(solution)/shard_map/ppermute | solution.py:272
  61.4 43.5 %copy-start.8 = (f32[256,1024]{1,0:T(8,128)}, f32[256,1024]{1,0:T(8,128)S(1)}, u32[]{:S(2)}) copy-start(f32[256,1024]{1,0:T(8,128)S(1)} %collective-permute-done.8.refs_16_.refs_7_) | copy-start | bytes 3145732
  61.4 38.2 %collective-permute-start.9 = (f32[256,1024]{1,0:T(8,128)S(1)}, f32[256,1024]{1,0:T(8,128)S(1)}, u32[]{:S(2)}, u32[]{:S(2)}) collective-permute-start(f32[256,1024]{1,0:T(8,128)S(1)} %collective-permute-done.2.refs_14_.refs_5_), channel_id=1, source_target_pairs={{8,0},{10,2},{12,4},{14,6},{16,8},{18,10},{20,12},{22,14},{24,16},... | collective-permute-start | bytes 3145736 | tf_op jit(solution)/shard_map/ppermute | solution.py:272
  64.4 39.2 %collective-permute-start.3 = (f32[256,1024]{1,0:T(8,128)S(1)}, f32[256,1024]{1,0:T(8,128)S(1)}, u32[]{:S(2)}, u32[]{:S(2)}) collective-permute-start(f32[256,1024]{1,0:T(8,128)S(1)} %collective-permute-done.2.refs_14_.refs_5_), channel_id=1, source_target_pairs={{2,0},{4,2},{6,4},{0,6},{10,8},{12,10},{14,12},{8,14},{18,16},{20,... | collective-permute-start | bytes 3145736 | tf_op jit(solution)/shard_map/ppermute | solution.py:272
  64.5 43.4 %copy-start.10 = (f32[256,1024]{1,0:T(8,128)}, f32[256,1024]{1,0:T(8,128)S(1)}, u32[]{:S(2)}) copy-start(f32[256,1024]{1,0:T(8,128)S(1)} %collective-permute-done.6.refs_15_.refs_6_) | copy-start | bytes 3145732
  64.5 40.4 %collective-permute-start.11 = (f32[256,1024]{1,0:T(8,128)S(1)}, f32[256,1024]{1,0:T(8,128)S(1)}, u32[]{:S(2)}, u32[]{:S(2)}) collective-permute-start(f32[256,1024]{1,0:T(8,128)S(1)} %collective-permute-done.6.refs_15_.refs_6_), channel_id=1, source_target_pairs={{24,0},{26,2},{28,4},{30,6},{0,8},{2,10},{4,12},{6,14},{8,16},{10,... | collective-permute-start | bytes 3145736 | tf_op jit(solution)/shard_map/ppermute | solution.py:272
  64.6 41.2 %collective-permute-start.7 = (f32[256,1024]{1,0:T(8,128)S(1)}, f32[256,1024]{1,0:T(8,128)S(1)}, u32[]{:S(2)}, u32[]{:S(2)}) collective-permute-start(f32[256,1024]{1,0:T(8,128)S(1)} %collective-permute-done.6.refs_15_.refs_6_), channel_id=1, source_target_pairs={{6,0},{0,2},{2,4},{4,6},{14,8},{8,10},{10,12},{12,14},{22,16},{16,... | collective-permute-start | bytes 3145736 | tf_op jit(solution)/shard_map/ppermute | solution.py:272
  99.6 28.9 %collective-permute-start.13 = (f32[256,1024]{1,0:T(8,128)S(1)}, f32[256,1024]{1,0:T(8,128)}, u32[]{:S(2)}, u32[]{:S(2)}) collective-permute-start(f32[256,1024]{1,0:T(8,128)S(1)} %collective-permute-done.refs_12_.refs_3_), channel_id=1, source_target_pairs={{8,0},{10,2},{12,4},{14,6},{16,8},{18,10},{20,12},{22,14},{24,16},... | collective-permute-start | bytes 3145736 | tf_op jit(solution)/shard_map/ppermute | solution.py:272
  103.6 26.6 %collective-permute-start.12 = (f32[256,1024]{1,0:T(8,128)}, f32[256,1024]{1,0:T(8,128)}, u32[]{:S(2)}, u32[]{:S(2)}) collective-permute-start(f32[256,1024]{1,0:T(8,128)} %copy-done.5), channel_id=1, source_target_pairs={{2,0},{4,2},{6,4},{0,6},{10,8},{12,10},{14,12},{8,14},{18,16},{20,... | collective-permute-start | bytes 3145736 | tf_op jit(solution)/shard_map/ppermute | solution.py:272
  105.8 13.0 %collective-permute-start.14 = (f32[128,1024]{1,0:T(8,128)}, f32[128,1024]{1,0:T(8,128)}, u32[]{:S(2)}, u32[]{:S(2)}) collective-permute-start(f32[128,1024]{1,0:T(8,128)} %slice.8), channel_id=1, source_target_pairs={{6,0},{0,2},{2,4},{4,6},{14,8},{8,10},{10,12},{12,14},{22,16},{16,... | collective-permute-start | bytes 1572872 | tf_op jit(solution)/shard_map/ppermute | solution.py:272
  107.9 11.0 %collective-permute-start.15 = (f32[128,1024]{1,0:T(8,128)}, f32[128,1024]{1,0:T(8,128)}, u32[]{:S(2)}, u32[]{:S(2)}) collective-permute-start(f32[128,1024]{1,0:T(8,128)} %slice.9), channel_id=1, source_target_pairs={{24,0},{26,2},{28,4},{30,6},{0,8},{2,10},{4,12},{6,14},{8,16},{10,... | collective-permute-start | bytes 1572872 | tf_op jit(solution)/shard_map/ppermute | solution.py:272
  139.0 21.4 %collective-permute-start.16 = (f32[256,1024]{1,0:T(8,128)}, f32[256,1024]{1,0:T(8,128)S(1)}, u32[]{:S(2)}, u32[]{:S(2)}) collective-permute-start(f32[256,1024]{1,0:T(8,128)} %shard_map.174.mine.cross_mine), channel_id=1, source_target_pairs={{0,1},{1,0},{2,3},{3,2},{4,5},{5,4},{6,7},{7,6},{8,9},{9,8},{10,11... | collective-permute-start | bytes 3145736 | tf_op jit(solution)/shard_map/ppermute | solution.py:276
  196.7 4.1 %collective-permute-start.17 = (f32[16,128,128]{2,1,0:T(8,128)S(1)}, f32[16,128,128]{2,1,0:T(8,128)S(1)}, u32[]{:S(2)}, u32[]{:S(2)}) collective-permute-start(f32[16,128,128]{2,1,0:T(8,128)S(1)} %all_to_all.10.mine.turned_mine), channel_id=1, source_target_pairs={{0,1},{1,0},{2,3},{3,2},{4,5},{5,4},{6,7},{7,6},{8,9},{9,8},{10,11... | collective-permute-start | bytes 3145736 | tf_op jit(solution)/shard_map/ppermute | solution.py:276
  212.1 2.2 collective-permute-start.18
  241.3 2.5 collective-permute-start.19
  270.2 4.5 %collective-permute-start.20 = (f32[16,192,128]{2,1,0:T(8,128)S(1)}, f32[16,192,128]{2,1,0:T(8,128)S(1)}, u32[]{:S(2)}, u32[]{:S(2)}) collective-permute-start(f32[16,192,128]{2,1,0:T(8,128)S(1)} %all_to_all.11.mine), channel_id=1, source_target_pairs={{0,1},{1,0},{2,3},{3,2},{4,5},{5,4},{6,7},{7,6},{8,9},{9,8},{10,11... | collective-permute-start | bytes 4718600 | tf_op jit(solution)/shard_map/ppermute | solution.py:276
  (17 other events, 266.4 us)
Sparse Core Ops, SparseCore 0:
  9.8 41.6 all-gather.2
  53.9 154.0 all-gather.4

commit v2 on v1

v2 whole, which is shorter than its diff:
```python
import functools

import jax
import jax.numpy as jnp
from jax import lax
from jax.experimental import pallas as pl
from jax.experimental.pallas import tpu as pltpu
from jax.sharding import PartitionSpec as P

BLK = 256
LANES = 128
SIDE = 4
CHIPS = SIDE * SIDE
TILE = 512
GROUP = 4
PER_CORE = 4
VMEM_LIMIT = 60 * 1024 * 1024
EAST, WEST, SOUTH, NORTH = (0, 1), (0, 3), (1, 0), (3, 0)


def split(value):
    high = value.astype(jnp.bfloat16)
    return high, (value - high.astype(jnp.float32)).astype(jnp.bfloat16)


def mxu(left, right):
    return jnp.dot(left, right, preferred_element_type=jnp.float32)


def three_pass(left_high, left_low, rights, widths):
    total, at = None, 0
    for ref, width in zip(rights, widths):
        for start in range(0, width, BLK):
            size = min(BLK, width - start)
            high, low = split(ref[start:start + size, :])
            ours = left_high[:, at:at + size]
            term = mxu(ours, high) + mxu(ours, low) + mxu(left_low[:, at:at + size], high)
            total = term if total is None else total + term
            at += size
    return total


def stacked_pass(left, rights, widths):
    rows = left.shape[0] // 2
    total, at = None, 0
    for ref, width in zip(rights, widths):
        for start in range(0, width, BLK):
            size = min(BLK, width - start)
            high, low = split(ref[start:start + size, :])
            both = mxu(left[:, at:at + size], high)
            term = both[:rows] + both[rows:] + mxu(left[:rows, at:at + size], low)
            total = term if total is None else total + term
            at += size
    return total


def cross_kernel(widths, has_base, has_turn, spots, core, *refs):
    count = len(widths)
    lefts, rights, rest = refs[:count], refs[count:2 * count], refs[2 * count:]
    base = rest[0] if has_base else None
    out, *turning, left_high, left_low = rest[1:] if has_base else rest

    @pl.when(pl.program_id(0) == 0)
    def _():
        at = 0
        for ref, width in zip(lefts, widths):
            left_high[:, at:at + width], left_low[:, at:at + width] = split(ref[...])
            at += width

    total = three_pass(left_high, left_low, rights, widths)
    out[...] = base[...] - total if has_base else -total
    if has_turn:
        halves_of(out, core[0], *turning)


def cross_sum(base, left, spots, core, rights, has_turn=False):
    rows, columns = left.shape[0], rights[0].shape[1]
    widths = tuple(array.shape[0] for array in rights)
    tile = pl.BlockSpec((rows, TILE), lambda n, spots, core: (0, n))
    in_specs = [
        pl.BlockSpec((rows, width), functools.partial(lambda j, n, spots, core: (0, spots[j]), j))
        for j, width in enumerate(widths)
    ] + [pl.BlockSpec((width, TILE), lambda n, spots, core: (0, n)) for width in widths]
    operands = [spots, core] + [left] * len(rights) + list(rights)
    if base is not None:
        in_specs.append(tile)
        operands.append(base)
    out_specs, shapes = [tile], [(rows, columns)]
    if has_turn:
        out_specs += [pl.BlockSpec((TILE // LANES, rows // 2, LANES), lambda n, spots, core: (n, 0, 0))] * 2
        shapes += [(columns // LANES, rows // 2, LANES)] * 2
    return pl.pallas_call(
        functools.partial(cross_kernel, widths, base is not None, has_turn),
        grid_spec=pltpu.PrefetchScalarGridSpec(
            num_scalar_prefetch=2,
            grid=(columns // TILE,),
            in_specs=in_specs,
            out_specs=out_specs,
            scratch_shapes=[pltpu.VMEM((rows, sum(widths)), jnp.bfloat16)] * 2,
        ),
        out_shape=[jax.ShapeDtypeStruct(shape, jnp.float32) for shape in shapes],
        compiler_params=pltpu.CompilerParams(vmem_limit_bytes=VMEM_LIMIT),
        cost_estimate=pl.CostEstimate(flops=1000, bytes_accessed=1000, transcendentals=0),
    )(*operands)


def in_order(is_first, mine, theirs):
    return jnp.where(is_first, mine, theirs), jnp.where(is_first, theirs, mine)


def inner_kernel(pieces, widths, spots, core, mine, theirs, *refs):
    rights, base = refs[:len(widths)], refs[len(widths)]
    out, left = refs[-2:]

    @pl.when(pl.program_id(0) == 0)
    def _():
        is_first = core[0] == 0
        at = 0
        for j, halves in enumerate(pieces):
            both = in_order(is_first, mine[spots[j]], theirs[spots[j]])
            for half in halves:
                left[:LANES, at:at + LANES], left[LANES:, at:at + LANES] = split(both[half].T)
                at += LANES

    out[...] = base[...] - stacked_pass(left, rights, widths)


def inner_sum(base, mine, theirs, spots, core, pieces, rights):
    rows, columns = base.shape
    widths = tuple(array.shape[0] for array in rights)
    whole = pl.BlockSpec(mine.shape, lambda n, spots, core: (0, 0, 0))
    tile = pl.BlockSpec((rows, TILE), lambda n, spots, core: (0, n))
    return pl.pallas_call(
        functools.partial(inner_kernel, pieces, widths),
        grid_spec=pltpu.PrefetchScalarGridSpec(
            num_scalar_prefetch=2,
            grid=(columns // TILE,),
            in_specs=[whole, whole]
            + [pl.BlockSpec((width, TILE), lambda n, spots, core: (0, n)) for width in widths]
            + [tile],
            out_specs=tile,
            scratch_shapes=[pltpu.VMEM((2 * rows, sum(widths)), jnp.bfloat16)],
        ),
        out_shape=jax.ShapeDtypeStruct(base.shape, jnp.float32),
        compiler_params=pltpu.CompilerParams(vmem_limit_bytes=VMEM_LIMIT),
        cost_estimate=pl.CostEstimate(flops=1000, bytes_accessed=1000, transcendentals=0),
    )(spots, core, mine, theirs, *rights, base)


def pick_kernel(spots, core, root, mine, theirs, high, low):
    for j in range(spots.shape[0]):
        spot, at = spots[j], slice(j * BLK, (j + 1) * BLK)

        @pl.when(spot < CHIPS)
        def _():
            high[:, at], low[:, at] = split(root[:, pl.ds(pl.multiple_of(spot * BLK, BLK), BLK)])

        @pl.when(spot >= CHIPS)
        def _():
            block = spot - CHIPS
            columns = pl.ds(pl.multiple_of((block % PER_CORE) * BLK, BLK), BLK)
            ours = block // PER_CORE == core[0]
            high[:, at], low[:, at] = split(jnp.where(ours, mine[:, columns], theirs[:, columns]))


def pick(spots, core, root, cross, cross_theirs):
    shape = jax.ShapeDtypeStruct((root.shape[0], spots.shape[0] * BLK), jnp.bfloat16)
    space = pl.BlockSpec(memory_space=pltpu.VMEM)
    scalars = [pl.BlockSpec(memory_space=pltpu.SMEM)] * 2
    return pl.pallas_call(
        pick_kernel,
        in_specs=scalars + [space] * 3,
        out_specs=[space] * 2,
        out_shape=[shape] * 2,
        compiler_params=pltpu.CompilerParams(vmem_limit_bytes=VMEM_LIMIT),
        cost_estimate=pl.CostEstimate(flops=0, bytes_accessed=20 * root.size, transcendentals=0),
    )(spots, core, root, cross, cross_theirs)


def halves_of(out, core, keep, give):
    rows = keep.shape[1]
    for ref, half in ((keep, core), (give, 1 - core)):
        for k in range(ref.shape[0]):
            ref[k] = out[pl.ds(pl.multiple_of(half * rows, rows), rows), k * LANES:(k + 1) * LANES]


def column_kernel(spots, core, top_high, top_low, *refs):
    step = pl.program_id(0)
    lefts, (lower, out_top, out_low, keep, give, high, low) = refs[:4 * GROUP], refs[4 * GROUP:]
    turns, turn_others, inners, inner_others = [lefts[kind * GROUP:(kind + 1) * GROUP] for kind in range(4)]
    top = out_top.shape[0]
    high[:top, :], low[:top, :] = top_high[...], top_low[...]

    for q in range(GROUP):
        spot, at = spots[step * GROUP + q], q * BLK

        def store(columns, value):
            high[top:, columns], low[top:, columns] = split(value)

        @pl.when(spot < CHIPS)
        def _():
            for half, value in enumerate(in_order(core[0] == 0, turns[q][0], turn_others[q][0])):
                store(slice(at + half * LANES, at + (half + 1) * LANES), value.T)

        @pl.when(spot >= CHIPS)
        def _():
            ours = (spot - CHIPS) // PER_CORE == core[0]
            store(slice(at, at + BLK), jnp.where(ours, inners[q][...], inner_others[q][...]))

    for n in range(0, lower.shape[1], TILE):
        columns = slice(n, n + TILE)
        total = three_pass(high, low, [lower.at[:, columns]], [lower.shape[0]])

        @pl.when(step == 0)
        def _():
            out_top[:, columns], out_low[:, columns] = -total[:top], -total[top:]

        @pl.when(step > 0)
        def _():
            out_top[:, columns] -= total[:top]
            out_low[:, columns] -= total[top:]

    @pl.when(step == pl.num_programs(0) - 1)
    def _():
        halves_of(out_top, core[0], keep.at[:, :LANES], give.at[:, :LANES])
        halves_of(out_low, core[0], keep.at[:, LANES:], give.at[:, LANES:])


def column_sum(spots, core, picked, turned, turned_theirs, inner, inner_theirs, lower):
    top, low, columns = picked[0].shape[0], inner.shape[0], lower.shape[1]

    def listed(shape, place):
        return [
            pl.BlockSpec(shape, functools.partial(lambda q, k, spots, core: place(spots[k * GROUP + q]), q))
            for q in range(GROUP)
        ]

    def block(spot):
        return jnp.maximum(spot - CHIPS, 0) % PER_CORE

    in_specs = [pl.BlockSpec((top, GROUP * BLK), lambda k, spots, core: (0, k))] * 2
    in_specs += 2 * listed((1, LANES, LANES), lambda spot: (jnp.minimum(spot, CHIPS - 1), 0, 0))
    in_specs += 2 * listed((low, BLK), lambda spot: (0, block(spot)))
    in_specs.append(pl.BlockSpec((GROUP * BLK, columns), lambda k, spots, core: (k, 0)))
    operands = [x for x in (turned, turned_theirs, inner, inner_theirs) for _ in range(GROUP)]
    shapes = [(top, columns), (low, columns)] + [(columns // LANES, (top + low) // 2, LANES)] * 2
    return pl.pallas_call(
        column_kernel,
        grid_spec=pltpu.PrefetchScalarGridSpec(
            num_scalar_prefetch=2,
            grid=(spots.shape[0] // GROUP,),
            in_specs=in_specs,
            out_specs=[
                pl.BlockSpec(shape, functools.partial(lambda size, k, spots, core: (0,) * size, len(shape)))
                for shape in shapes
            ],
            scratch_shapes=[pltpu.VMEM((top + low, GROUP * BLK), jnp.bfloat16)] * 2,
        ),
        out_shape=[jax.ShapeDtypeStruct(shape, jnp.float32) for shape in shapes],
        compiler_params=pltpu.CompilerParams(vmem_limit_bytes=VMEM_LIMIT),
        cost_estimate=pl.CostEstimate(flops=1000, bytes_accessed=1000, transcendentals=0),
    )(spots, core, *picked, *operands, lower)


def last_kernel(spots, core, mine, theirs, lower, base, out, high, low):
    @pl.when(pl.program_id(0) == 0)
    def _():
        is_first = core[0] == 0
        for j in range(spots.shape[0]):
            spot = spots[j]

            def store(parts):
                for half, value in enumerate(parts):
                    at = slice(j * BLK + half * LANES, j * BLK + (half + 1) * LANES)
                    high[:, at], low[:, at] = split(value.T)

            @pl.when(spot < CHIPS)
            def _():
                store(in_order(is_first, mine[spot, :LANES, :], theirs[spot, :LANES, :]))

            @pl.when(spot >= CHIPS)
            def _():
                chips = (2 * (spot - CHIPS), 2 * (spot - CHIPS) + 1)
                store([jnp.concatenate(in_order(is_first, mine[c, LANES:, :], theirs[c, LANES:, :])) for c in chips])

    out[...] = base[...] - three_pass(high, low, [lower], [lower.shape[0]])


def last_sum(base, mine, theirs, spots, core, lower):
    rows, columns = base.shape
    whole = pl.BlockSpec(mine.shape, lambda n, spots, core: (0, 0, 0))
    tile = pl.BlockSpec((rows, TILE), lambda n, spots, core: (0, n))
    return pl.pallas_call(
        last_kernel,
        grid_spec=pltpu.PrefetchScalarGridSpec(
            num_scalar_prefetch=2,
            grid=(columns // TILE,),
            in_specs=[whole, whole, pl.BlockSpec((lower.shape[0], TILE), lambda n, spots, core: (0, n)), tile],
            out_specs=tile,
            scratch_shapes=[pltpu.VMEM((rows, lower.shape[0]), jnp.bfloat16)] * 2,
        ),
        out_shape=jax.ShapeDtypeStruct(base.shape, jnp.float32),
        compiler_params=pltpu.CompilerParams(vmem_limit_bytes=VMEM_LIMIT),
        cost_estimate=pl.CostEstimate(flops=1000, bytes_accessed=1000, transcendentals=0),
    )(spots, core, mine, theirs, lower, base)


def after(value, *others):
    return lax.optimization_barrier((value,) + others)[0]


def pull(value, way):
    pairs = []
    for target in range(CHIPS):
        y, x = divmod(target, SIDE)
        pairs.append((((y + way[0]) % SIDE) * SIDE + (x + way[1]) % SIDE, target))
    return lax.ppermute(value, "row", pairs)


def other_core(value):
    return lax.ppermute(value, "col", [(0, 1), (1, 0)])


def turn(core, keep, give):
    sent = jnp.concatenate(in_order(core == 0, keep, other_core(give)), axis=0)
    return lax.all_to_all(sent, "row", split_axis=0, concat_axis=0, tiled=True)


def first_round(own):
    return [pull(own, way) for way in (EAST, WEST, SOUTH, NORTH)]


def second_round(near, *gates):
    e, w, s, n = near
    es = pull(after(s, e, *gates), EAST)
    wn = pull(after(n, w, *gates), WEST)
    sw = pull(after(w, s, *gates), SOUTH)
    ne = pull(after(e, n, *gates), NORTH)
    return es, wn, sw, ne


def third_round(diagonal, *gates):
    es, wn, sw, ne = diagonal
    ees = pull(after(es, *gates), EAST)
    wwn = pull(after(wn, *gates), WEST)
    sse = pull(after(es, sw, *gates), SOUTH)
    nnw = pull(after(wn, ne, *gates), NORTH)
    return ees, wwn, sse, nnw


def fourth_round(near, third, *gates):
    e, w, s, n = near
    ees, wwn, sse, nnw = third
    half = e.shape[0] // 2
    first = pull(after(nnw[:half], wwn, *gates), WEST)
    second = pull(after(wwn[half:], nnw, *gates), NORTH)
    return pull(after(e, ees, *gates), EAST), pull(after(s, sse, *gates), SOUTH), first, second


PLACES = [
    [(0, 0), EAST, WEST, SOUTH, NORTH, (1, 1), (3, 3), (1, 3), (3, 1)],
    [(1, 2), (3, 2), (2, 1), (2, 3)],
    [(0, 2), (2, 0), (2, 2), (2, 2)],
]
WHOLE = (0, 1)
HALVES = [[WHOLE] * 9, [WHOLE] * 4, [WHOLE, WHOLE, (0,), (1,)]]


def body(root_inverse, panel_one, diag_one, panel_two, diag_two, structure):
    place = lax.axis_index("row")
    core = lax.axis_index("col").astype(jnp.int32)
    core_vector = core[None]
    blocks = structure[0, 0]
    own_upper, own_lower = panel_one[0], panel_two[0, 0]

    def chips(places):
        down = jnp.array([spot[0] for spot in places], jnp.int32)
        right = jnp.array([spot[1] for spot in places], jnp.int32)
        return ((place // SIDE + down) % SIDE) * SIDE + (place % SIDE + right) % SIDE

    halves = sum(HALVES, [])
    every_spots = chips(sum(PLACES, []))
    late_spots = chips(PLACES[2]) * jnp.array([1, 1, 2, 2], jnp.int32) + jnp.array([0, 0, 0, 1], jnp.int32)

    root_rows = lax.all_gather(root_inverse, ("leaf", "col"), axis=1, tiled=True)

    near = first_round(own_upper)
    diagonal = second_round(near)
    third = third_round(diagonal)
    lower = lax.all_gather(after(own_lower, *near), "row", axis=0, tiled=True)
    early = [own_upper, *near, *diagonal]
    cross, = cross_sum(None, root_rows, every_spots[:9], core_vector, early)
    fourth = fourth_round(near, third)
    cross, = cross_sum(cross, root_rows, every_spots[9:13], core_vector, third)
    cross, keep, give = cross_sum(cross, root_rows, late_spots, core_vector, fourth, True)
    turned = turn(core, keep, give)
    picked = pick(blocks, core_vector, root_rows, cross, other_core(cross))
    turned = after(turned, *picked)
    turned_theirs = other_core(turned)
    upper = [*early, *third, *fourth]
    inner = inner_sum(diag_one[0], turned, turned_theirs, every_spots, core_vector, sum(HALVES, []), upper)

    top, low, keep, give = column_sum(
        blocks, core_vector, picked, turned, turned_theirs, inner, other_core(inner), lower
    )
    turned = turn(core, keep, give)
    inner_low = last_sum(diag_two[0, 0], turned, other_core(turned), blocks, core_vector, lower)
    return cross[None], inner[None], top[None, None], low[None, None], inner_low[None, None]


def solution(mesh):
    in_specs = (
        P("row", ("leaf", "col")),
        P("leaf", "row", "col"),
        P("leaf", "row", "col"),
        P("leaf", None, "row", "col"),
        P("leaf", None, "row", "col"),
        P("leaf", None, None),
    )
    out_specs = (
        P("leaf", "row", "col"),
        P("leaf", "row", "col"),
        P("leaf", None, "row", "col"),
        P("leaf", None, "row", "col"),
        P("leaf", None, "row", "col"),
    )
    return jax.shard_map(body, mesh=mesh, in_specs=in_specs, out_specs=out_specs, check_vma=False)
```

time: 293 us -> 289 us (0.986)
  blocking collectives: 58 us -> 24.9 us
  waiting for transfers between devices: 101 us -> 125 us
  Pallas kernels: 67.5 us -> 71 us
    all_to_all x2 -> x1, blocking collectives: 58 us -> 24.9 us  [turn(): return lax.all_to_all(sent, 'row', split_axis=0, concat_axis=0, tiled=True)]
    all_to_all x0 -> x1, waiting for transfers between devices: none -> 21.6 us  [turn(): return lax.all_to_all(sent, 'row', split_axis=0, concat_axis=0, tiled=True)]
    ppermute x5 -> x6, starting transfers between devices: 23.1 us -> 17.7 us  [other_core(): return lax.ppermute(value, 'col', [(0, 1), (1, 0)])]
    all_to_all x0 -> x1, starting transfers between devices: none -> 5.08 us  [turn(): return lax.all_to_all(sent, 'row', split_axis=0, concat_axis=0, tiled=True)]
    pallas_call x7, Pallas kernels: 67.5 us -> 71 us  [the longest x3 22.9 us: cross_sum(): pl.pallas_call(functools.partial(cross_kernel, widths, base is not None,...]
    unnamed x52 -> x48, local copies, waits for them, and re-layouts: 3.96 us -> 5.87 us
    ppermute x5 -> x6, waiting for transfers between devices: 10.5 us -> 10.8 us  [other_core(): return lax.ppermute(value, 'col', [(0, 1), (1, 0)])]
  transfers between devices with their start and end apart: 23 -> 25, of which waited for: 15 -> 14; matrix products, arithmetic and copies ran while one was open for 1% -> 2% of each run, Pallas kernels for 14% -> 14%
where the time goes in v2:
time: 289 us; the launch traced here: 288 us
  waiting for transfers between devices  125 us (43%)
  Pallas kernels  71 us (25%)
  starting transfers between devices  40.7 us (14%)
  blocking collectives  24.9 us (9%)
  between operations  14.3 us (5%)
  local copies, waits for them, and re-layouts  8.18 us (3%)
  other arithmetic  4.17 us (1%)
    ppermute x16, waiting for transfers between devices, pull(): return lax.ppermute(value, 'row', pairs)  92.1 us
    all_to_all x1, blocking collectives, turn(): return lax.all_to_all(sent, 'row', split_axis=0, concat_axis=0, tiled=True)  24.9 us
    pallas_call x3, Pallas kernels, cross_sum(): pl.pallas_call(functools.partial(cross_kernel, widths, base is not None,...  22.9 us
    all_to_all x1, waiting for transfers between devices, turn(): return lax.all_to_all(sent, 'row', split_axis=0, concat_axis=0, tiled=True)  21.6 us
    pallas_call x1, Pallas kernels, column_sum(): pl.pallas_call(column_kernel, grid_spec=pltpu.PrefetchScalarGridSpec(num_...  20.1 us
    ppermute x16, starting transfers between devices, pull(): return lax.ppermute(value, 'row', pairs)  17.8 us
    ppermute x6, starting transfers between devices, other_core(): return lax.ppermute(value, 'col', [(0, 1), (1, 0)])  17.7 us
    pallas_call x1, Pallas kernels, last_sum(): pl.pallas_call(last_kernel, grid_spec=pltpu.PrefetchScalarGridSpec(num_sc...  11.4 us
  transfers between devices with their start and end apart: 25, of which 14 were waited for; matrix products, arithmetic and copies ran while one was open for 2% of the time, Pallas kernels for 14%

profile of v2, /device:TPU:225, one launch (start us, length us, event | category | flops | bytes accessed | tf_op | source)
XLA Modules:
  0.0 288.4 jit_solution(11088865962836780652)
XLA Ops:
  7.9 2.6 collective-permute-start
  10.5 2.7 collective-permute-start.1
  13.2 19.4 %collective-permute-done.refs_10_.refs_1_ = f32[256,1024]{1,0:T(8,128)S(1)} collective-permute-done((f32[256,1024]{1,0:T(8,128)}, f32[256,1024]{1,0:T(8,128)S(1)}, u32[]{:S(2)}, u32[]{:S(2)}) %collective-permute-start) | collective-permute-done | bytes 1048608 | tf_op jit(solution)/shard_map/ppermute | solution.py:317
  32.6 2.4 collective-permute-done.1.refs_12_.refs_3_
  35.1 3.1 %collective-permute-done.5.refs_11_.refs_2_ = f32[256,1024]{1,0:T(8,128)S(1)} collective-permute-done((f32[256,1024]{1,0:T(8,128)}, f32[256,1024]{1,0:T(8,128)S(1)}, u32[]{:S(2)}, u32[]{:S(2)}) %collective-permute-start.5) | collective-permute-done | bytes 1048608 | tf_op jit(solution)/shard_map/ppermute | solution.py:317
  38.2 2.5 collective-permute-start.2
  40.7 1.5 collective-permute-start.11
  42.1 18.6 %collective-permute-done.2.refs_14_.refs_5_ = f32[256,1024]{1,0:T(8,128)S(1)} collective-permute-done((f32[256,1024]{1,0:T(8,128)S(1)}, f32[256,1024]{1,0:T(8,128)S(1)}, u32[]{:S(2)}, u32[]{:S(2)}) %collective-permute-start.2) | collective-permute-done | bytes 1048608 | tf_op jit(solution)/shard_map/ppermute | solution.py:317
  60.8 1.8 collective-permute-done.6.refs_16_.refs_7_
  63.6 1.5 collective-permute-start.7
  66.7 35.2 %collective-permute-done.7.refs_6_.refs_11_ = f32[256,1024]{1,0:T(8,128)S(1)} collective-permute-done((f32[256,1024]{1,0:T(8,128)S(1)}, f32[256,1024]{1,0:T(8,128)S(1)}, u32[]{:S(2)}, u32[]{:S(2)}) %collective-permute-start.7) | collective-permute-done | bytes 1048608 | tf_op jit(solution)/shard_map/ppermute | solution.py:317
  102.0 3.5 %collective-permute-start.8 = (f32[256,1024]{1,0:T(8,128)}, f32[256,1024]{1,0:T(8,128)}, u32[]{:S(2)}, u32[]{:S(2)}) collective-permute-start(f32[256,1024]{1,0:T(8,128)} %copy-done.9), channel_id=1, source_target_pairs={{8,0},{10,2},{12,4},{14,6},{16,8},{18,10},{20,12},{22,14},{24,16},... | collective-permute-start | bytes 3145736 | tf_op jit(solution)/shard_map/ppermute | solution.py:317
  110.8 10.9 %shard_map.155.refs_8_ = f32[256,1024]{1,0:T(8,128)} custom-call(s32[9]{0:T(128)} %bitcast.27, s32[1]{0:T(128)} %bitcast.core, f32[256,4096]{1,0:T(8,128)} %all-gather.3.cloned.1.call-done.refs_0_.refs_1_.refs_2_.refs_3_.refs_4_.refs_5_.refs_6_.refs_7_.refs_8_.root, ...), custom_call_target="tpu_custom_call" | custom-call | flops 1000 | bytes 1000 | tf_op jit(solution)/shard_map/pallas_call | solution.py:92
  122.3 6.1 %shard_map.156.refs_8_ = f32[256,1024]{1,0:T(8,128)} custom-call(s32[4]{0:T(128)} %slice.14.spots, s32[1]{0:T(128)} %bitcast.core, f32[256,4096]{1,0:T(8,128)} %all-gather.3.cloned.1.call-done.refs_0_.refs_1_.refs_2_.refs_3_.refs_4_.refs_5_.refs_6_.refs_7_.refs_8_.root, ...), custom_call_target="tpu_custom_call" | custom-call | flops 1000 | bytes 1000 | tf_op jit(solution)/shard_map/pallas_call | solution.py:92
  128.5 7.6 %collective-permute-done.8.refs_5_.refs_14_ = f32[256,1024]{1,0:T(8,128)} collective-permute-done((f32[256,1024]{1,0:T(8,128)}, f32[256,1024]{1,0:T(8,128)}, u32[]{:S(2)}, u32[]{:S(2)}) %collective-permute-start.8) | collective-permute-done | bytes 1048608 | tf_op jit(solution)/shard_map/ppermute | solution.py:317
  136.1 3.8 %collective-permute-done.4.refs_4_.refs_13_ = f32[256,1024]{1,0:T(8,128)} collective-permute-done((f32[256,1024]{1,0:T(8,128)}, f32[256,1024]{1,0:T(8,128)}, u32[]{:S(2)}, u32[]{:S(2)}) %collective-permute-start.4) | collective-permute-done | bytes 1048608 | tf_op jit(solution)/shard_map/ppermute | solution.py:317
  139.9 5.9 %shard_map.157 = (f32[256,1024]{1,0:T(8,128)}, f32[8,128,128]{2,1,0:T(8,128)}, f32[8,128,128]{2,1,0:T(8,128)}) custom-call(s32[4]{0:T(128)} %fusion.6.spots, s32[1]{0:T(128)} %bitcast.core, f32[256,4096]{1,0:T(8,128)} %all-gather.3.cloned.1.call-done.refs_0_.refs_1_.refs_2_.refs_3_.refs_4_.refs_5_.refs_6_.refs_7_.refs_8_.root, ...), custom_call_target="tpu_custom_call" | custom-call | flops 1000 | bytes 1000 | tf_op jit(solution)/shard_map/pallas_call | solution.py:92
  145.8 13.5 %collective-permute-start.16 = (f32[8,128,128]{2,1,0:T(8,128)}, f32[8,128,128]{2,1,0:T(8,128)S(1)}, u32[]{:S(2)}, u32[]{:S(2)}) collective-permute-start(f32[8,128,128]{2,1,0:T(8,128)} %get-tuple-element.38), channel_id=1, source_target_pairs={{0,1},{1,0},{2,3},{3,2},{4,5},{5,4},{6,7},{7,6},{8,9},{9,8},{10,11... | collective-permute-start | bytes 1572872 | tf_op jit(solution)/shard_map/ppermute | solution.py:321
  159.4 1.6 collective-permute-done.16
  163.3 5.1 %all-to-all-start = ((f32[16,128,128]{2,1,0:T(8,128)}), f32[16,128,128]{2,1,0:T(8,128)S(1)}, u32[]{:S(2)}, u32[]{:S(2)}) async-start(f32[16,128,128]{2,1,0:T(8,128)} %pad_maximum_fusion.1), calls=%async_computation | async-start | bytes 2097152 | tf_op jit(solution)/shard_map/all_to_all | solution.py:326
  169.3 5.9 %shard_map.158 = (bf16[256,4096]{1,0:T(8,128)(2,1)}, bf16[256,4096]{1,0:T(8,128)(2,1)}) custom-call(s32[16]{0:T(128)} %bitcast.24, s32[1]{0:T(128)} %bitcast.core, f32[256,4096]{1,0:T(8,128)} %all-gather.3.cloned.1.call-done.refs_0_.refs_1_.refs_2_.refs_3_.refs_4_.refs_5_.refs_6_.refs_7_.refs_8_.root, f32[256,1024]{1,0:T(8,128)} %get-tuple-element.36.mine, ...), custom_call_target="tpu_custom_call" | custom-call | bytes 20971520 | tf_op jit(solution)/shard_map/pallas_call | solution.py:170
  175.3 21.6 %all-to-all-done.mine.refs_0_.refs_1_.refs_2_.refs_3_ = f32[16,128,128]{2,1,0:T(8,128)S(1)} async-done(((f32[16,128,128]{2,1,0:T(8,128)}), f32[16,128,128]{2,1,0:T(8,128)S(1)}, u32[]{:S(2)}, u32[]{:S(2)}) %all-to-all-start) | async-done | bytes 1048608 | tf_op jit(solution)/shard_map/all_to_all | solution.py:326
  196.9 1.5 collective-permute-start.18
  198.4 2.3 collective-permute-done.18.theirs.refs_4_.refs_5_.refs_6_.refs_7_
  201.6 10.6 %shard_map.159.refs_8_.refs_9_.refs_10_.refs_11_ = f32[128,1024]{1,0:T(8,128)} custom-call(s32[17]{0:T(128)} %copy-done.17, s32[1]{0:T(128)} %bitcast.core, f32[16,128,128]{2,1,0:T(8,128)} %copy-done, f32[16,128,128]{2,1,0:T(8,128)} %copy-done.1, f32[256,1024]{1,0:T(8,128)} %bitcast.18, f32[256,1024]{1,0:T(8,128)} %copy-done.8, f32[256,1024]{1,0:T(8,128)} %copy-done.10, ...), custom_call_target="tpu_custom_call" | custom-call | flops 1000 | bytes 1000 | tf_op jit(solution)/shard_map/pallas_call | solution.py:133
  212.9 1.8 collective-permute-done.19.refs_12_.refs_13_.refs_14_.refs_15_
  215.4 20.1 %shard_map.160 = (f32[256,1024]{1,0:T(8,128)}, f32[128,1024]{1,0:T(8,128)}, f32[8,192,128]{2,1,0:T(8,128)}, f32[8,192,128]{2,1,0:T(8,128)}) custom-call(s32[16]{0:T(128)} %bitcast.25, s32[1]{0:T(128)} %bitcast.core, bf16[256,4096]{1,0:T(8,128)(2,1)} %get-tuple-element.39.top_high, bf16[256,4096]{1,0:T(8,128)(2,1)} %get-tuple-element.40.top_low, ...), custom_call_target="tpu_custom_call" | custom-call | flops 1000 | bytes 1000 | tf_op jit(solution)/shard_map/pallas_call | solution.py:247
  236.0 2.1 collective-permute-done.20
  239.6 24.9 %all_to_all.10.mine = f32[16,192,128]{2,1,0:T(8,128)S(1)} all-to-all(f32[16,192,128]{2,1,0:T(8,128)S(1)} %pad_maximum_fusion), channel_id=1, replica_groups=mesh['leaf'=8,'row'=16,'col'=2] {'row'}, dimensions={0} | all-to-all | bytes 3145728 | tf_op jit(solution)/shard_map/all_to_all | solution.py:326
  264.5 1.5 collective-permute-start.21
  266.0 3.0 %collective-permute-done.21.theirs = f32[16,192,128]{2,1,0:T(8,128)S(1)} collective-permute-done((f32[16,192,128]{2,1,0:T(8,128)S(1)}, f32[16,192,128]{2,1,0:T(8,128)S(1)}, u32[]{:S(2)}, u32[]{:S(2)}) %collective-permute-start.21) | collective-permute-done | bytes 1572896 | tf_op jit(solution)/shard_map/ppermute | solution.py:321
  270.2 11.4 %shard_map.161 = f32[128,1024]{1,0:T(8,128)} custom-call(s32[16]{0:T(128)} %bitcast.26, s32[1]{0:T(128)} %bitcast.core, f32[16,192,128]{2,1,0:T(8,128)} %copy-done.5, f32[16,192,128]{2,1,0:T(8,128)} %copy-done.15, f32[4096,1024]{1,0:T(8,128)} %all-gather.5.cloned.1.call-done.refs_16_.lower, f32[128,1024]{1,0:T(8,128)} %bitcast.22), custom_call_target="tpu_custom_call" | custom-call | flops 1000 | bytes 1000 | tf_op jit(solution)/shard_map/pallas_call | solution.py:293
  (85 shorter events, 18.0 us)
Async XLA Ops:
  7.2 103.6 %all-gather.3.cloned.1.call-start = ((), (), s32[]{:S(2)}) async-start(), calls=%async_computation.2 | async-start | bytes 4456448 | tf_op jit(solution)/shard_map/all_gather | solution.py:385
  7.9 206.7 %all-gather.5.cloned.1.call-start = ((), (), s32[]{:S(2)}) async-start(), calls=%async_computation.3 | async-start | bytes 17825792 | tf_op jit(solution)/shard_map/all_gather | solution.py:390
  7.9 24.7 %collective-permute-start = (f32[256,1024]{1,0:T(8,128)}, f32[256,1024]{1,0:T(8,128)S(1)}, u32[]{:S(2)}, u32[]{:S(2)}) collective-permute-start(f32[256,1024]{1,0:T(8,128)} %bitcast.13), channel_id=1, source_target_pairs={{2,0},{4,2},{6,4},{0,6},{10,8},{12,10},{14,12},{8,14},{18,16},{20,... | collective-permute-start | bytes 3145736 | tf_op jit(solution)/shard_map/ppermute | solution.py:317
  10.5 24.6 %collective-permute-start.1 = (f32[256,1024]{1,0:T(8,128)}, f32[256,1024]{1,0:T(8,128)S(1)}, u32[]{:S(2)}, u32[]{:S(2)}) collective-permute-start(f32[256,1024]{1,0:T(8,128)} %bitcast.14), channel_id=1, source_target_pairs={{8,0},{10,2},{12,4},{14,6},{16,8},{18,10},{20,12},{22,14},{24,16},... | collective-permute-start | bytes 3145736 | tf_op jit(solution)/shard_map/ppermute | solution.py:317
  13.2 24.9 %collective-permute-start.5 = (f32[256,1024]{1,0:T(8,128)}, f32[256,1024]{1,0:T(8,128)S(1)}, u32[]{:S(2)}, u32[]{:S(2)}) collective-permute-start(f32[256,1024]{1,0:T(8,128)} %bitcast.15), channel_id=1, source_target_pairs={{6,0},{0,2},{2,4},{4,6},{14,8},{8,10},{10,12},{12,14},{22,16},{16,... | collective-permute-start | bytes 3145736 | tf_op jit(solution)/shard_map/ppermute | solution.py:317
  13.2 24.9 %collective-permute-start.9 = (f32[256,1024]{1,0:T(8,128)}, f32[256,1024]{1,0:T(8,128)}, u32[]{:S(2)}, u32[]{:S(2)}) collective-permute-start(f32[256,1024]{1,0:T(8,128)} %bitcast.16), channel_id=1, source_target_pairs={{24,0},{26,2},{28,4},{30,6},{0,8},{2,10},{4,12},{6,14},{8,16},{10,... | collective-permute-start | bytes 3145736 | tf_op jit(solution)/shard_map/ppermute | solution.py:317
  32.6 32.8 %copy-start.8 = (f32[256,1024]{1,0:T(8,128)}, f32[256,1024]{1,0:T(8,128)S(1)}, u32[]{:S(2)}) copy-start(f32[256,1024]{1,0:T(8,128)S(1)} %collective-permute-done.refs_10_.refs_1_) | copy-start | bytes 3145732
  38.2 27.3 %copy-start.10 = (f32[256,1024]{1,0:T(8,128)}, f32[256,1024]{1,0:T(8,128)S(1)}, u32[]{:S(2)}) copy-start(f32[256,1024]{1,0:T(8,128)S(1)} %collective-permute-done.5.refs_11_.refs_2_) | copy-start | bytes 3145732
  38.2 72.0 %copy-start.22 = (s32[17]{0:T(128)S(1)}, s32[17]{0:T(128)}, u32[]{:S(2)}) copy-start(s32[17]{0:T(128)} %constant.79.clone) | copy-start | bytes 208
  38.2 72.0 %copy-start.23 = (s32[17]{0:T(128)S(1)}, s32[17]{0:T(128)}, u32[]{:S(2)}) copy-start(s32[17]{0:T(128)} %constant.80.clone) | copy-start | bytes 208
  38.2 22.6 %collective-permute-start.2 = (f32[256,1024]{1,0:T(8,128)S(1)}, f32[256,1024]{1,0:T(8,128)S(1)}, u32[]{:S(2)}, u32[]{:S(2)}) collective-permute-start(f32[256,1024]{1,0:T(8,128)S(1)} %collective-permute-done.1.refs_12_.refs_3_), channel_id=1, source_target_pairs={{2,0},{4,2},{6,4},{0,6},{10,8},{12,10},{14,12},{8,14},{18,16},{20,... | collective-permute-start | bytes 3145736 | tf_op jit(solution)/shard_map/ppermute | solution.py:317
  40.7 21.9 %collective-permute-start.6 = (f32[256,1024]{1,0:T(8,128)S(1)}, f32[256,1024]{1,0:T(8,128)S(1)}, u32[]{:S(2)}, u32[]{:S(2)}) collective-permute-start(f32[256,1024]{1,0:T(8,128)S(1)} %collective-permute-done.5.refs_11_.refs_2_), channel_id=1, source_target_pairs={{8,0},{10,2},{12,4},{14,6},{16,8},{18,10},{20,12},{22,14},{24,16},... | collective-permute-start | bytes 3145736 | tf_op jit(solution)/shard_map/ppermute | solution.py:317
  40.7 24.8 %collective-permute-start.10 = (f32[256,1024]{1,0:T(8,128)}, f32[256,1024]{1,0:T(8,128)S(1)}, u32[]{:S(2)}, u32[]{:S(2)}) collective-permute-start(f32[256,1024]{1,0:T(8,128)} %collective-permute-done.9.refs_13_.refs_4_), channel_id=1, source_target_pairs={{6,0},{0,2},{2,4},{4,6},{14,8},{8,10},{10,12},{12,14},{22,16},{16,... | collective-permute-start | bytes 3145736 | tf_op jit(solution)/shard_map/ppermute | solution.py:317
  40.7 24.8 %collective-permute-start.11 = (f32[256,1024]{1,0:T(8,128)S(1)}, f32[256,1024]{1,0:T(8,128)S(1)}, u32[]{:S(2)}, u32[]{:S(2)}) collective-permute-start(f32[256,1024]{1,0:T(8,128)S(1)} %collective-permute-done.refs_10_.refs_1_), channel_id=1, source_target_pairs={{24,0},{26,2},{28,4},{30,6},{0,8},{2,10},{4,12},{6,14},{8,16},{10,... | collective-permute-start | bytes 3145736 | tf_op jit(solution)/shard_map/ppermute | solution.py:317
  60.8 46.6 %copy-start.11 = (f32[256,1024]{1,0:T(8,128)}, f32[256,1024]{1,0:T(8,128)S(1)}, u32[]{:S(2)}) copy-start(f32[256,1024]{1,0:T(8,128)S(1)} %collective-permute-done.2.refs_14_.refs_5_) | copy-start | bytes 3145732
  63.6 38.4 %collective-permute-start.7 = (f32[256,1024]{1,0:T(8,128)S(1)}, f32[256,1024]{1,0:T(8,128)S(1)}, u32[]{:S(2)}, u32[]{:S(2)}) collective-permute-start(f32[256,1024]{1,0:T(8,128)S(1)} %collective-permute-done.2.refs_14_.refs_5_), channel_id=1, source_target_pairs={{8,0},{10,2},{12,4},{14,6},{16,8},{18,10},{20,12},{22,14},{24,16},... | collective-permute-start | bytes 3145736 | tf_op jit(solution)/shard_map/ppermute | solution.py:317
  65.1 40.4 %collective-permute-start.3 = (f32[256,1024]{1,0:T(8,128)S(1)}, f32[256,1024]{1,0:T(8,128)S(1)}, u32[]{:S(2)}, u32[]{:S(2)}) collective-permute-start(f32[256,1024]{1,0:T(8,128)S(1)} %collective-permute-done.2.refs_14_.refs_5_), channel_id=1, source_target_pairs={{2,0},{4,2},{6,4},{0,6},{10,8},{12,10},{14,12},{8,14},{18,16},{20,... | collective-permute-start | bytes 3145736 | tf_op jit(solution)/shard_map/ppermute | solution.py:317
  65.5 42.8 %copy-start.13 = (f32[256,1024]{1,0:T(8,128)}, f32[256,1024]{1,0:T(8,128)S(1)}, u32[]{:S(2)}) copy-start(f32[256,1024]{1,0:T(8,128)S(1)} %collective-permute-done.10.refs_15_.refs_6_) | copy-start | bytes 3145732
  65.5 41.9 %copy-start.14 = (f32[256,1024]{1,0:T(8,128)}, f32[256,1024]{1,0:T(8,128)S(1)}, u32[]{:S(2)}) copy-start(f32[256,1024]{1,0:T(8,128)S(1)} %collective-permute-done.11.refs_17_.refs_8_) | copy-start | bytes 3145732
  65.5 41.9 %collective-permute-start.12 = (f32[256,1024]{1,0:T(8,128)S(1)}, f32[256,1024]{1,0:T(8,128)S(1)}, u32[]{:S(2)}, u32[]{:S(2)}) collective-permute-start(f32[256,1024]{1,0:T(8,128)S(1)} %collective-permute-done.10.refs_15_.refs_6_), channel_id=1, source_target_pairs={{24,0},{26,2},{28,4},{30,6},{0,8},{2,10},{4,12},{6,14},{8,16},{10,... | collective-permute-start | bytes 3145736 | tf_op jit(solution)/shard_map/ppermute | solution.py:317
  66.7 41.6 %collective-permute-start.13 = (f32[256,1024]{1,0:T(8,128)S(1)}, f32[256,1024]{1,0:T(8,128)S(1)}, u32[]{:S(2)}, u32[]{:S(2)}) collective-permute-start(f32[256,1024]{1,0:T(8,128)S(1)} %collective-permute-done.10.refs_15_.refs_6_), channel_id=1, source_target_pairs={{6,0},{0,2},{2,4},{4,6},{14,8},{8,10},{10,12},{12,14},{22,16},{16,... | collective-permute-start | bytes 3145736 | tf_op jit(solution)/shard_map/ppermute | solution.py:317
  102.0 34.1 %collective-permute-start.8 = (f32[256,1024]{1,0:T(8,128)}, f32[256,1024]{1,0:T(8,128)}, u32[]{:S(2)}, u32[]{:S(2)}) collective-permute-start(f32[256,1024]{1,0:T(8,128)} %copy-done.9), channel_id=1, source_target_pairs={{8,0},{10,2},{12,4},{14,6},{16,8},{18,10},{20,12},{22,14},{24,16},... | collective-permute-start | bytes 3145736 | tf_op jit(solution)/shard_map/ppermute | solution.py:317
  106.4 33.5 %collective-permute-start.4 = (f32[256,1024]{1,0:T(8,128)}, f32[256,1024]{1,0:T(8,128)}, u32[]{:S(2)}, u32[]{:S(2)}) collective-permute-start(f32[256,1024]{1,0:T(8,128)} %copy-done.8), channel_id=1, source_target_pairs={{2,0},{4,2},{6,4},{0,6},{10,8},{12,10},{14,12},{8,14},{18,16},{20,... | collective-permute-start | bytes 3145736 | tf_op jit(solution)/shard_map/ppermute | solution.py:317
  108.3 20.2 %collective-permute-start.14 = (f32[128,1024]{1,0:T(8,128)}, f32[128,1024]{1,0:T(8,128)}, u32[]{:S(2)}, u32[]{:S(2)}) collective-permute-start(f32[128,1024]{1,0:T(8,128)} %slice.16), channel_id=1, source_target_pairs={{6,0},{0,2},{2,4},{4,6},{14,8},{8,10},{10,12},{12,14},{22,16},{16,... | collective-permute-start | bytes 1572872 | tf_op jit(solution)/shard_map/ppermute | solution.py:317
  109.7 18.7 %collective-permute-start.15 = (f32[128,1024]{1,0:T(8,128)}, f32[128,1024]{1,0:T(8,128)}, u32[]{:S(2)}, u32[]{:S(2)}) collective-permute-start(f32[128,1024]{1,0:T(8,128)} %slice.17), channel_id=1, source_target_pairs={{24,0},{26,2},{28,4},{30,6},{0,8},{2,10},{4,12},{6,14},{8,16},{10,... | collective-permute-start | bytes 1572872 | tf_op jit(solution)/shard_map/ppermute | solution.py:317
  145.8 15.2 %collective-permute-start.16 = (f32[8,128,128]{2,1,0:T(8,128)}, f32[8,128,128]{2,1,0:T(8,128)S(1)}, u32[]{:S(2)}, u32[]{:S(2)}) collective-permute-start(f32[8,128,128]{2,1,0:T(8,128)} %get-tuple-element.38), channel_id=1, source_target_pairs={{0,1},{1,0},{2,3},{3,2},{4,5},{5,4},{6,7},{7,6},{8,9},{9,8},{10,11... | collective-permute-start | bytes 1572872 | tf_op jit(solution)/shard_map/ppermute | solution.py:321
  159.3 9.1 %collective-permute-start.17 = (f32[256,1024]{1,0:T(8,128)}, f32[256,1024]{1,0:T(8,128)S(1)}, u32[]{:S(2)}, u32[]{:S(2)}) collective-permute-start(f32[256,1024]{1,0:T(8,128)} %get-tuple-element.36.mine), channel_id=1, source_target_pairs={{0,1},{1,0},{2,3},{3,2},{4,5},{5,4},{6,7},{7,6},{8,9},{9,8},{10,11... | collective-permute-start | bytes 3145736 | tf_op jit(solution)/shard_map/ppermute | solution.py:321
  163.3 33.6 %all-to-all-start = ((f32[16,128,128]{2,1,0:T(8,128)}), f32[16,128,128]{2,1,0:T(8,128)S(1)}, u32[]{:S(2)}, u32[]{:S(2)}) async-start(f32[16,128,128]{2,1,0:T(8,128)} %pad_maximum_fusion.1), calls=%async_computation | async-start | bytes 2097152 | tf_op jit(solution)/shard_map/all_to_all | solution.py:326
  196.9 3.8 %collective-permute-start.18 = (f32[16,128,128]{2,1,0:T(8,128)S(1)}, f32[16,128,128]{2,1,0:T(8,128)S(1)}, u32[]{:S(2)}, u32[]{:S(2)}) collective-permute-start(f32[16,128,128]{2,1,0:T(8,128)S(1)} %all-to-all-done.mine.refs_0_.refs_1_.refs_2_.refs_3_), channel_id=1, source_target_pairs={{0,1},{1,0},{2,3},{3,2},{4,5},{5,4},{6,7},{7,6},{8,9},{9,8},{10,11... | collective-permute-start | bytes 3145736 | tf_op jit(solution)/shard_map/ppermute | solution.py:321
  212.2 2.4 collective-permute-start.19
  235.6 2.6 collective-permute-start.20
  264.5 4.5 %collective-permute-start.21 = (f32[16,192,128]{2,1,0:T(8,128)S(1)}, f32[16,192,128]{2,1,0:T(8,128)S(1)}, u32[]{:S(2)}, u32[]{:S(2)}) collective-permute-start(f32[16,192,128]{2,1,0:T(8,128)S(1)} %all_to_all.10.mine), channel_id=1, source_target_pairs={{0,1},{1,0},{2,3},{3,2},{4,5},{5,4},{6,7},{7,6},{8,9},{9,8},{10,11... | collective-permute-start | bytes 4718600 | tf_op jit(solution)/shard_map/ppermute | solution.py:321
  (17 other events, 132.1 us)
Sparse Core Ops, SparseCore 0:
  9.8 41.6 all-gather.2
  53.9 156.8 all-gather.4

commit v3 on v2

--- a/solution.py
+++ b/solution.py
@@ -35,20 +35,6 @@
             high, low = split(ref[start:start + size, :])
             ours = left_high[:, at:at + size]
             term = mxu(ours, high) + mxu(ours, low) + mxu(left_low[:, at:at + size], high)
-            total = term if total is None else total + term
-            at += size
-    return total
-
-
-def stacked_pass(left, rights, widths):
-    rows = left.shape[0] // 2
-    total, at = None, 0
-    for ref, width in zip(rights, widths):
-        for start in range(0, width, BLK):
-            size = min(BLK, width - start)
-            high, low = split(ref[start:start + size, :])
-            both = mxu(left[:, at:at + size], high)
-            term = both[:rows] + both[rows:] + mxu(left[:rows, at:at + size], low)
             total = term if total is None else total + term
             at += size
     return total
@@ -108,43 +94,47 @@
     return jnp.where(is_first, mine, theirs), jnp.where(is_first, theirs, mine)
 
 
-def inner_kernel(pieces, widths, spots, core, mine, theirs, *refs):
-    rights, base = refs[:len(widths)], refs[len(widths)]
-    out, left = refs[-2:]
+def inner_kernel(pieces, spots, core, mine, theirs, *refs):
+    rights, (base, out, turned_high, turned_low) = refs[:len(pieces)], refs[len(pieces):]
 
     @pl.when(pl.program_id(0) == 0)
     def _():
-        is_first = core[0] == 0
-        at = 0
-        for j, halves in enumerate(pieces):
-            both = in_order(is_first, mine[spots[j]], theirs[spots[j]])
-            for half in halves:
-                left[:LANES, at:at + LANES], left[LANES:, at:at + LANES] = split(both[half].T)
-                at += LANES
-
-    out[...] = base[...] - stacked_pass(left, rights, widths)
+        for chip in range(CHIPS):
+            for half, value in enumerate(in_order(core[0] == 0, mine[chip], theirs[chip])):
+                at = slice(chip * BLK + half * LANES, chip * BLK + (half + 1) * LANES)
+                turned_high[:, at], turned_low[:, at] = split(value.T)
+
+    total = base[...]
+    for j, (ref, halves) in enumerate(zip(rights, pieces)):
+        high, low = split(ref[...])
+        columns = pl.ds(pl.multiple_of(spots[j] * BLK + halves[0] * LANES, LANES), ref.shape[0])
+        ours = turned_high[:, columns]
+        total -= mxu(ours, high) + mxu(ours, low) + mxu(turned_low[:, columns], high)
+    out[...] = total
 
 
 def inner_sum(base, mine, theirs, spots, core, pieces, rights):
     rows, columns = base.shape
-    widths = tuple(array.shape[0] for array in rights)
+    depth = 2 * mine.shape[0] * mine.shape[1]
     whole = pl.BlockSpec(mine.shape, lambda n, spots, core: (0, 0, 0))
     tile = pl.BlockSpec((rows, TILE), lambda n, spots, core: (0, n))
-    return pl.pallas_call(
-        functools.partial(inner_kernel, pieces, widths),
+    part = pl.BlockSpec((rows, depth), lambda n, spots, core: (0, 0))
+    out, *turned = pl.pallas_call(
+        functools.partial(inner_kernel, pieces),
         grid_spec=pltpu.PrefetchScalarGridSpec(
             num_scalar_prefetch=2,
             grid=(columns // TILE,),
             in_specs=[whole, whole]
-            + [pl.BlockSpec((width, TILE), lambda n, spots, core: (0, n)) for width in widths]
+            + [pl.BlockSpec((array.shape[0], TILE), lambda n, spots, core: (0, n)) for array in rights]
             + [tile],
-            out_specs=tile,
-            scratch_shapes=[pltpu.VMEM((2 * rows, sum(widths)), jnp.bfloat16)],
+            out_specs=[tile, part, part],
         ),
-        out_shape=jax.ShapeDtypeStruct(base.shape, jnp.float32),
+        out_shape=[jax.ShapeDtypeStruct(base.shape, jnp.float32)]
+        + [jax.ShapeDtypeStruct((rows, depth), jnp.bfloat16)] * 2,
         compiler_params=pltpu.CompilerParams(vmem_limit_bytes=VMEM_LIMIT),
         cost_estimate=pl.CostEstimate(flops=1000, bytes_accessed=1000, transcendentals=0),
     )(spots, core, mine, theirs, *rights, base)
+    return out, turned
 
 
 def pick_kernel(spots, core, root, mine, theirs, high, low):
@@ -187,25 +177,23 @@
 def column_kernel(spots, core, top_high, top_low, *refs):
     step = pl.program_id(0)
     lefts, (lower, out_top, out_low, keep, give, high, low) = refs[:4 * GROUP], refs[4 * GROUP:]
-    turns, turn_others, inners, inner_others = [lefts[kind * GROUP:(kind + 1) * GROUP] for kind in range(4)]
+    turned_high, turned_low, inners, inner_others = [lefts[kind * GROUP:(kind + 1) * GROUP] for kind in range(4)]
     top = out_top.shape[0]
     high[:top, :], low[:top, :] = top_high[...], top_low[...]
 
     for q in range(GROUP):
         spot, at = spots[step * GROUP + q], q * BLK
 
-        def store(columns, value):
-            high[top:, columns], low[top:, columns] = split(value)
-
         @pl.when(spot < CHIPS)
         def _():
-            for half, value in enumerate(in_order(core[0] == 0, turns[q][0], turn_others[q][0])):
-                store(slice(at + half * LANES, at + (half + 1) * LANES), value.T)
+            columns = slice(at, at + BLK)
+            high[top:, columns], low[top:, columns] = turned_high[q][...], turned_low[q][...]
 
         @pl.when(spot >= CHIPS)
         def _():
             ours = (spot - CHIPS) // PER_CORE == core[0]
-            store(slice(at, at + BLK), jnp.where(ours, inners[q][...], inner_others[q][...]))
+            columns = slice(at, at + BLK)
+            high[top:, columns], low[top:, columns] = split(jnp.where(ours, inners[q][...], inner_others[q][...]))
 
     for n in range(0, lower.shape[1], TILE):
         columns = slice(n, n + TILE)
@@ -226,7 +214,7 @@
         halves_of(out_low, core[0], keep.at[:, LANES:], give.at[:, LANES:])
 
 
-def column_sum(spots, core, picked, turned, turned_theirs, inner, inner_theirs, lower):
+def column_sum(spots, core, picked, turned, inner, inner_theirs, lower):
     top, low, columns = picked[0].shape[0], inner.shape[0], lower.shape[1]
 
     def listed(shape, place):
@@ -239,10 +227,10 @@
         return jnp.maximum(spot - CHIPS, 0) % PER_CORE
 
     in_specs = [pl.BlockSpec((top, GROUP * BLK), lambda k, spots, core: (0, k))] * 2
-    in_specs += 2 * listed((1, LANES, LANES), lambda spot: (jnp.minimum(spot, CHIPS - 1), 0, 0))
+    in_specs += 2 * listed((low, BLK), lambda spot: (0, jnp.minimum(spot, CHIPS - 1)))
     in_specs += 2 * listed((low, BLK), lambda spot: (0, block(spot)))
     in_specs.append(pl.BlockSpec((GROUP * BLK, columns), lambda k, spots, core: (k, 0)))
-    operands = [x for x in (turned, turned_theirs, inner, inner_theirs) for _ in range(GROUP)]
+    operands = [x for x in (*turned, inner, inner_theirs) for _ in range(GROUP)]
     shapes = [(top, columns), (low, columns)] + [(columns // LANES, (top + low) // 2, LANES)] * 2
     return pl.pallas_call(
         column_kernel,
@@ -268,20 +256,13 @@
         is_first = core[0] == 0
         for j in range(spots.shape[0]):
             spot = spots[j]
-
-            def store(parts):
-                for half, value in enumerate(parts):
-                    at = slice(j * BLK + half * LANES, j * BLK + (half + 1) * LANES)
-                    high[:, at], low[:, at] = split(value.T)
-
-            @pl.when(spot < CHIPS)
-            def _():
-                store(in_order(is_first, mine[spot, :LANES, :], theirs[spot, :LANES, :]))
-
-            @pl.when(spot >= CHIPS)
-            def _():
-                chips = (2 * (spot - CHIPS), 2 * (spot - CHIPS) + 1)
-                store([jnp.concatenate(in_order(is_first, mine[c, LANES:, :], theirs[c, LANES:, :])) for c in chips])
+            chip, first_low = jnp.minimum(spot, CHIPS - 1), jnp.maximum(2 * (spot - CHIPS), 0)
+            parts = in_order(is_first, mine[chip, :LANES, :], theirs[chip, :LANES, :])
+            for half, value in enumerate(parts):
+                c = first_low + half
+                lower_rows = jnp.concatenate(in_order(is_first, mine[c, LANES:, :], theirs[c, LANES:, :]))
+                at = slice(j * BLK + half * LANES, j * BLK + (half + 1) * LANES)
+                high[:, at], low[:, at] = split(jnp.where(spot < CHIPS, value, lower_rows).T)
 
     out[...] = base[...] - three_pass(high, low, [lower], [lower.shape[0]])
 
@@ -398,10 +379,10 @@
     turned = after(turned, *picked)
     turned_theirs = other_core(turned)
     upper = [*early, *third, *fourth]
-    inner = inner_sum(diag_one[0], turned, turned_theirs, every_spots, core_vector, sum(HALVES, []), upper)
+    inner, turned_parts = inner_sum(diag_one[0], turned, turned_theirs, every_spots, core_vector, sum(HALVES, []), upper)
 
     top, low, keep, give = column_sum(
-        blocks, core_vector, picked, turned, turned_theirs, inner, other_core(inner), lower
+        blocks, core_vector, picked, turned_parts, inner, other_core(inner), lower
     )
     turned = turn(core, keep, give)
     inner_low = last_sum(diag_two[0, 0], turned, other_core(turned), blocks, core_vector, lower)

time: 289 us -> 287 us (level)
  no operation moved by 1% of the time
where the time goes in v3:
time: 287 us
  waiting for transfers between devices  125 us (44%)
  Pallas kernels  69.3 us (24%)
  starting transfers between devices  40.6 us (14%)
  blocking collectives  24.9 us (9%)
  between operations  14.3 us (5%)
  local copies, waits for them, and re-layouts  8.16 us (3%)
  other arithmetic  4.16 us (1%)
    ppermute x16, waiting for transfers between devices, pull(): return lax.ppermute(value, 'row', pairs)  92.1 us
    all_to_all x1, blocking collectives, turn(): return lax.all_to_all(sent, 'row', split_axis=0, concat_axis=0, tiled=True)  24.9 us
    pallas_call x3, Pallas kernels, cross_sum(): pl.pallas_call(functools.partial(cross_kernel, widths, base is not None,...  22.9 us
    all_to_all x1, waiting for transfers between devices, turn(): return lax.all_to_all(sent, 'row', split_axis=0, concat_axis=0, tiled=True)  21.6 us
    pallas_call x1, Pallas kernels, column_sum(): pl.pallas_call(column_kernel, grid_spec=pltpu.PrefetchScalarGridSpec(num_...  19.2 us
    ppermute x6, starting transfers between devices, other_core(): return lax.ppermute(value, 'col', [(0, 1), (1, 0)])  17.8 us
    ppermute x16, starting transfers between devices, pull(): return lax.ppermute(value, 'row', pairs)  17.7 us
    pallas_call x1, Pallas kernels, inner_sum(): pl.pallas_call(functools.partial(inner_kernel, pieces), grid_spec=pltpu.P...  11.1 us
  transfers between devices with their start and end apart: 25, of which 14 were waited for; matrix products, arithmetic and copies ran while one was open for 2% of the time, Pallas kernels for 14%

profile of v3, /device:TPU:225, one launch (start us, length us, event | category | flops | bytes accessed | tf_op | source)
XLA Modules:
  0.0 286.8 jit_solution(4310978233140610469)
XLA Ops:
  7.9 2.6 collective-permute-start
  10.5 2.7 collective-permute-start.1
  13.2 19.4 %collective-permute-done.refs_10_.refs_1_ = f32[256,1024]{1,0:T(8,128)S(1)} collective-permute-done((f32[256,1024]{1,0:T(8,128)}, f32[256,1024]{1,0:T(8,128)S(1)}, u32[]{:S(2)}, u32[]{:S(2)}) %collective-permute-start) | collective-permute-done | bytes 1048608 | tf_op jit(solution)/shard_map/ppermute | solution.py:298
  32.6 2.4 collective-permute-done.1.refs_12_.refs_3_
  35.1 3.1 %collective-permute-done.5.refs_11_.refs_2_ = f32[256,1024]{1,0:T(8,128)S(1)} collective-permute-done((f32[256,1024]{1,0:T(8,128)}, f32[256,1024]{1,0:T(8,128)S(1)}, u32[]{:S(2)}, u32[]{:S(2)}) %collective-permute-start.5) | collective-permute-done | bytes 1048608 | tf_op jit(solution)/shard_map/ppermute | solution.py:298
  38.2 2.5 collective-permute-start.2
  40.7 1.5 collective-permute-start.11
  42.1 18.6 %collective-permute-done.2.refs_14_.refs_5_ = f32[256,1024]{1,0:T(8,128)S(1)} collective-permute-done((f32[256,1024]{1,0:T(8,128)S(1)}, f32[256,1024]{1,0:T(8,128)S(1)}, u32[]{:S(2)}, u32[]{:S(2)}) %collective-permute-start.2) | collective-permute-done | bytes 1048608 | tf_op jit(solution)/shard_map/ppermute | solution.py:298
  60.8 1.8 collective-permute-done.6.refs_16_.refs_7_
  63.6 1.5 collective-permute-start.7
  66.7 35.3 %collective-permute-done.7.refs_6_.refs_11_ = f32[256,1024]{1,0:T(8,128)S(1)} collective-permute-done((f32[256,1024]{1,0:T(8,128)S(1)}, f32[256,1024]{1,0:T(8,128)S(1)}, u32[]{:S(2)}, u32[]{:S(2)}) %collective-permute-start.7) | collective-permute-done | bytes 1048608 | tf_op jit(solution)/shard_map/ppermute | solution.py:298
  102.0 3.5 %collective-permute-start.8 = (f32[256,1024]{1,0:T(8,128)}, f32[256,1024]{1,0:T(8,128)}, u32[]{:S(2)}, u32[]{:S(2)}) collective-permute-start(f32[256,1024]{1,0:T(8,128)} %copy-done.8), channel_id=1, source_target_pairs={{8,0},{10,2},{12,4},{14,6},{16,8},{18,10},{20,12},{22,14},{24,16},... | collective-permute-start | bytes 3145736 | tf_op jit(solution)/shard_map/ppermute | solution.py:298
  110.8 10.9 %shard_map.155.refs_8_ = f32[256,1024]{1,0:T(8,128)} custom-call(s32[9]{0:T(128)} %bitcast.27, s32[1]{0:T(128)} %bitcast.core, f32[256,4096]{1,0:T(8,128)} %all-gather.3.cloned.1.call-done.refs_0_.refs_1_.refs_2_.refs_3_.refs_4_.refs_5_.refs_6_.refs_7_.refs_8_.root, ...), custom_call_target="tpu_custom_call" | custom-call | flops 1000 | bytes 1000 | tf_op jit(solution)/shard_map/pallas_call | solution.py:78
  122.3 6.1 %shard_map.156.refs_8_ = f32[256,1024]{1,0:T(8,128)} custom-call(s32[4]{0:T(128)} %slice.14.spots, s32[1]{0:T(128)} %bitcast.core, f32[256,4096]{1,0:T(8,128)} %all-gather.3.cloned.1.call-done.refs_0_.refs_1_.refs_2_.refs_3_.refs_4_.refs_5_.refs_6_.refs_7_.refs_8_.root, ...), custom_call_target="tpu_custom_call" | custom-call | flops 1000 | bytes 1000 | tf_op jit(solution)/shard_map/pallas_call | solution.py:78
  128.5 7.6 %collective-permute-done.8.refs_5_.refs_14_ = f32[256,1024]{1,0:T(8,128)} collective-permute-done((f32[256,1024]{1,0:T(8,128)}, f32[256,1024]{1,0:T(8,128)}, u32[]{:S(2)}, u32[]{:S(2)}) %collective-permute-start.8) | collective-permute-done | bytes 1048608 | tf_op jit(solution)/shard_map/ppermute | solution.py:298
  136.0 3.8 %collective-permute-done.4.refs_4_.refs_13_ = f32[256,1024]{1,0:T(8,128)} collective-permute-done((f32[256,1024]{1,0:T(8,128)}, f32[256,1024]{1,0:T(8,128)}, u32[]{:S(2)}, u32[]{:S(2)}) %collective-permute-start.4) | collective-permute-done | bytes 1048608 | tf_op jit(solution)/shard_map/ppermute | solution.py:298
  139.9 5.9 %shard_map.157 = (f32[256,1024]{1,0:T(8,128)}, f32[8,128,128]{2,1,0:T(8,128)}, f32[8,128,128]{2,1,0:T(8,128)}) custom-call(s32[4]{0:T(128)} %fusion.6.spots, s32[1]{0:T(128)} %bitcast.core, f32[256,4096]{1,0:T(8,128)} %all-gather.3.cloned.1.call-done.refs_0_.refs_1_.refs_2_.refs_3_.refs_4_.refs_5_.refs_6_.refs_7_.refs_8_.root, ...), custom_call_target="tpu_custom_call" | custom-call | flops 1000 | bytes 1000 | tf_op jit(solution)/shard_map/pallas_call | solution.py:78
  145.8 13.5 %collective-permute-start.16 = (f32[8,128,128]{2,1,0:T(8,128)}, f32[8,128,128]{2,1,0:T(8,128)S(1)}, u32[]{:S(2)}, u32[]{:S(2)}) collective-permute-start(f32[8,128,128]{2,1,0:T(8,128)} %get-tuple-element.41), channel_id=1, source_target_pairs={{0,1},{1,0},{2,3},{3,2},{4,5},{5,4},{6,7},{7,6},{8,9},{9,8},{10,11... | collective-permute-start | bytes 1572872 | tf_op jit(solution)/shard_map/ppermute | solution.py:302
  159.4 1.6 collective-permute-done.16
  163.2 5.1 %all-to-all-start = ((f32[16,128,128]{2,1,0:T(8,128)}), f32[16,128,128]{2,1,0:T(8,128)S(1)}, u32[]{:S(2)}, u32[]{:S(2)}) async-start(f32[16,128,128]{2,1,0:T(8,128)} %pad_maximum_fusion.1), calls=%async_computation | async-start | bytes 2097152 | tf_op jit(solution)/shard_map/all_to_all | solution.py:307
  169.3 5.9 %shard_map.158 = (bf16[256,4096]{1,0:T(8,128)(2,1)}, bf16[256,4096]{1,0:T(8,128)(2,1)}) custom-call(s32[16]{0:T(128)} %bitcast.24, s32[1]{0:T(128)} %bitcast.core, f32[256,4096]{1,0:T(8,128)} %all-gather.3.cloned.1.call-done.refs_0_.refs_1_.refs_2_.refs_3_.refs_4_.refs_5_.refs_6_.refs_7_.refs_8_.root, f32[256,1024]{1,0:T(8,128)} %get-tuple-element.39.mine, ...), custom_call_target="tpu_custom_call" | custom-call | bytes 20971520 | tf_op jit(solution)/shard_map/pallas_call | solution.py:160
  175.2 21.6 %all-to-all-done.mine = f32[16,128,128]{2,1,0:T(8,128)S(1)} async-done(((f32[16,128,128]{2,1,0:T(8,128)}), f32[16,128,128]{2,1,0:T(8,128)S(1)}, u32[]{:S(2)}, u32[]{:S(2)}) %all-to-all-start) | async-done | bytes 1048608 | tf_op jit(solution)/shard_map/all_to_all | solution.py:307
  196.8 1.5 collective-permute-start.18
  198.3 2.3 collective-permute-done.18.theirs
  201.6 11.1 %shard_map.159 = (f32[128,1024]{1,0:T(8,128)}, bf16[128,4096]{1,0:T(8,128)(2,1)}, bf16[128,4096]{1,0:T(8,128)(2,1)}) custom-call(s32[17]{0:T(128)} %copy-done.17, s32[1]{0:T(128)} %bitcast.core, f32[16,128,128]{2,1,0:T(8,128)} %copy-done.6, f32[16,128,128]{2,1,0:T(8,128)} %copy-done.15, f32[256,1024]{1,0:T(8,128)} %bitcast.18, f32[256,1024]{1,0:T(8,128)} %copy-done.7, ...), custom_call_target="tpu_custom_call" | custom-call | flops 1000 | bytes 1000 | tf_op jit(solution)/shard_map/pallas_call | solution.py:122
  213.4 1.7 collective-permute-done.19.refs_12_.refs_13_.refs_14_.refs_15_
  216.0 19.2 %shard_map.160 = (f32[256,1024]{1,0:T(8,128)}, f32[128,1024]{1,0:T(8,128)}, f32[8,192,128]{2,1,0:T(8,128)}, f32[8,192,128]{2,1,0:T(8,128)}) custom-call(s32[16]{0:T(128)} %bitcast.25, s32[1]{0:T(128)} %bitcast.core, bf16[256,4096]{1,0:T(8,128)(2,1)} %get-tuple-element.42.top_high, bf16[256,4096]{1,0:T(8,128)(2,1)} %get-tuple-element.43.top_low, ...), custom_call_target="tpu_custom_call" | custom-call | flops 1000 | bytes 1000 | tf_op jit(solution)/shard_map/pallas_call | solution.py:235
  235.6 2.1 collective-permute-done.20
  239.2 24.9 %all_to_all.10.mine = f32[16,192,128]{2,1,0:T(8,128)S(1)} all-to-all(f32[16,192,128]{2,1,0:T(8,128)S(1)} %pad_maximum_fusion), channel_id=1, replica_groups=mesh['leaf'=8,'row'=16,'col'=2] {'row'}, dimensions={0} | all-to-all | bytes 3145728 | tf_op jit(solution)/shard_map/all_to_all | solution.py:307
  264.1 1.5 collective-permute-start.21
  265.6 3.0 %collective-permute-done.21.theirs = f32[16,192,128]{2,1,0:T(8,128)S(1)} collective-permute-done((f32[16,192,128]{2,1,0:T(8,128)S(1)}, f32[16,192,128]{2,1,0:T(8,128)S(1)}, u32[]{:S(2)}, u32[]{:S(2)}) %collective-permute-start.21) | collective-permute-done | bytes 1572896 | tf_op jit(solution)/shard_map/ppermute | solution.py:302
  269.8 10.2 %shard_map.161 = f32[128,1024]{1,0:T(8,128)} custom-call(s32[16]{0:T(128)} %bitcast.26, s32[1]{0:T(128)} %bitcast.core, f32[16,192,128]{2,1,0:T(8,128)} %copy-done.3, f32[16,192,128]{2,1,0:T(8,128)} %copy-done.14, f32[4096,1024]{1,0:T(8,128)} %all-gather.5.cloned.1.call-done.refs_16_.lower, f32[128,1024]{1,0:T(8,128)} %bitcast.22), custom_call_target="tpu_custom_call" | custom-call | flops 1000 | bytes 1000 | tf_op jit(solution)/shard_map/pallas_call | solution.py:274
  (85 shorter events, 18.0 us)
Async XLA Ops:
  7.2 103.6 %all-gather.3.cloned.1.call-start = ((), (), s32[]{:S(2)}) async-start(), calls=%async_computation.2 | async-start | bytes 4456448 | tf_op jit(solution)/shard_map/all_gather | solution.py:366
  7.9 207.3 %all-gather.5.cloned.1.call-start = ((), (), s32[]{:S(2)}) async-start(), calls=%async_computation.3 | async-start | bytes 17825792 | tf_op jit(solution)/shard_map/all_gather | solution.py:371
  7.9 24.7 %collective-permute-start = (f32[256,1024]{1,0:T(8,128)}, f32[256,1024]{1,0:T(8,128)S(1)}, u32[]{:S(2)}, u32[]{:S(2)}) collective-permute-start(f32[256,1024]{1,0:T(8,128)} %bitcast.13), channel_id=1, source_target_pairs={{2,0},{4,2},{6,4},{0,6},{10,8},{12,10},{14,12},{8,14},{18,16},{20,... | collective-permute-start | bytes 3145736 | tf_op jit(solution)/shard_map/ppermute | solution.py:298
  10.5 24.6 %collective-permute-start.1 = (f32[256,1024]{1,0:T(8,128)}, f32[256,1024]{1,0:T(8,128)S(1)}, u32[]{:S(2)}, u32[]{:S(2)}) collective-permute-start(f32[256,1024]{1,0:T(8,128)} %bitcast.14), channel_id=1, source_target_pairs={{8,0},{10,2},{12,4},{14,6},{16,8},{18,10},{20,12},{22,14},{24,16},... | collective-permute-start | bytes 3145736 | tf_op jit(solution)/shard_map/ppermute | solution.py:298
  13.2 24.9 %collective-permute-start.5 = (f32[256,1024]{1,0:T(8,128)}, f32[256,1024]{1,0:T(8,128)S(1)}, u32[]{:S(2)}, u32[]{:S(2)}) collective-permute-start(f32[256,1024]{1,0:T(8,128)} %bitcast.15), channel_id=1, source_target_pairs={{6,0},{0,2},{2,4},{4,6},{14,8},{8,10},{10,12},{12,14},{22,16},{16,... | collective-permute-start | bytes 3145736 | tf_op jit(solution)/shard_map/ppermute | solution.py:298
  13.2 24.9 %collective-permute-start.9 = (f32[256,1024]{1,0:T(8,128)}, f32[256,1024]{1,0:T(8,128)}, u32[]{:S(2)}, u32[]{:S(2)}) collective-permute-start(f32[256,1024]{1,0:T(8,128)} %bitcast.16), channel_id=1, source_target_pairs={{24,0},{26,2},{28,4},{30,6},{0,8},{2,10},{4,12},{6,14},{8,16},{10,... | collective-permute-start | bytes 3145736 | tf_op jit(solution)/shard_map/ppermute | solution.py:298
  32.6 32.8 %copy-start.7 = (f32[256,1024]{1,0:T(8,128)}, f32[256,1024]{1,0:T(8,128)S(1)}, u32[]{:S(2)}) copy-start(f32[256,1024]{1,0:T(8,128)S(1)} %collective-permute-done.refs_10_.refs_1_) | copy-start | bytes 3145732
  38.2 27.3 %copy-start.9 = (f32[256,1024]{1,0:T(8,128)}, f32[256,1024]{1,0:T(8,128)S(1)}, u32[]{:S(2)}) copy-start(f32[256,1024]{1,0:T(8,128)S(1)} %collective-permute-done.5.refs_11_.refs_2_) | copy-start | bytes 3145732
  38.2 72.0 %copy-start.22 = (s32[17]{0:T(128)S(1)}, s32[17]{0:T(128)}, u32[]{:S(2)}) copy-start(s32[17]{0:T(128)} %constant.79.clone) | copy-start | bytes 208
  38.2 72.0 %copy-start.23 = (s32[17]{0:T(128)S(1)}, s32[17]{0:T(128)}, u32[]{:S(2)}) copy-start(s32[17]{0:T(128)} %constant.80.clone) | copy-start | bytes 208
  38.2 22.6 %collective-permute-start.2 = (f32[256,1024]{1,0:T(8,128)S(1)}, f32[256,1024]{1,0:T(8,128)S(1)}, u32[]{:S(2)}, u32[]{:S(2)}) collective-permute-start(f32[256,1024]{1,0:T(8,128)S(1)} %collective-permute-done.1.refs_12_.refs_3_), channel_id=1, source_target_pairs={{2,0},{4,2},{6,4},{0,6},{10,8},{12,10},{14,12},{8,14},{18,16},{20,... | collective-permute-start | bytes 3145736 | tf_op jit(solution)/shard_map/ppermute | solution.py:298
  40.7 21.9 %collective-permute-start.6 = (f32[256,1024]{1,0:T(8,128)S(1)}, f32[256,1024]{1,0:T(8,128)S(1)}, u32[]{:S(2)}, u32[]{:S(2)}) collective-permute-start(f32[256,1024]{1,0:T(8,128)S(1)} %collective-permute-done.5.refs_11_.refs_2_), channel_id=1, source_target_pairs={{8,0},{10,2},{12,4},{14,6},{16,8},{18,10},{20,12},{22,14},{24,16},... | collective-permute-start | bytes 3145736 | tf_op jit(solution)/shard_map/ppermute | solution.py:298
  40.7 24.8 %collective-permute-start.10 = (f32[256,1024]{1,0:T(8,128)}, f32[256,1024]{1,0:T(8,128)S(1)}, u32[]{:S(2)}, u32[]{:S(2)}) collective-permute-start(f32[256,1024]{1,0:T(8,128)} %collective-permute-done.9.refs_13_.refs_4_), channel_id=1, source_target_pairs={{6,0},{0,2},{2,4},{4,6},{14,8},{8,10},{10,12},{12,14},{22,16},{16,... | collective-permute-start | bytes 3145736 | tf_op jit(solution)/shard_map/ppermute | solution.py:298
  40.7 24.8 %collective-permute-start.11 = (f32[256,1024]{1,0:T(8,128)S(1)}, f32[256,1024]{1,0:T(8,128)S(1)}, u32[]{:S(2)}, u32[]{:S(2)}) collective-permute-start(f32[256,1024]{1,0:T(8,128)S(1)} %collective-permute-done.refs_10_.refs_1_), channel_id=1, source_target_pairs={{24,0},{26,2},{28,4},{30,6},{0,8},{2,10},{4,12},{6,14},{8,16},{10,... | collective-permute-start | bytes 3145736 | tf_op jit(solution)/shard_map/ppermute | solution.py:298
  60.8 46.5 %copy-start.10 = (f32[256,1024]{1,0:T(8,128)}, f32[256,1024]{1,0:T(8,128)S(1)}, u32[]{:S(2)}) copy-start(f32[256,1024]{1,0:T(8,128)S(1)} %collective-permute-done.2.refs_14_.refs_5_) | copy-start | bytes 3145732
  63.6 38.4 %collective-permute-start.7 = (f32[256,1024]{1,0:T(8,128)S(1)}, f32[256,1024]{1,0:T(8,128)S(1)}, u32[]{:S(2)}, u32[]{:S(2)}) collective-permute-start(f32[256,1024]{1,0:T(8,128)S(1)} %collective-permute-done.2.refs_14_.refs_5_), channel_id=1, source_target_pairs={{8,0},{10,2},{12,4},{14,6},{16,8},{18,10},{20,12},{22,14},{24,16},... | collective-permute-start | bytes 3145736 | tf_op jit(solution)/shard_map/ppermute | solution.py:298
  65.1 40.4 %collective-permute-start.3 = (f32[256,1024]{1,0:T(8,128)S(1)}, f32[256,1024]{1,0:T(8,128)S(1)}, u32[]{:S(2)}, u32[]{:S(2)}) collective-permute-start(f32[256,1024]{1,0:T(8,128)S(1)} %collective-permute-done.2.refs_14_.refs_5_), channel_id=1, source_target_pairs={{2,0},{4,2},{6,4},{0,6},{10,8},{12,10},{14,12},{8,14},{18,16},{20,... | collective-permute-start | bytes 3145736 | tf_op jit(solution)/shard_map/ppermute | solution.py:298
  65.4 42.8 %copy-start.12 = (f32[256,1024]{1,0:T(8,128)}, f32[256,1024]{1,0:T(8,128)S(1)}, u32[]{:S(2)}) copy-start(f32[256,1024]{1,0:T(8,128)S(1)} %collective-permute-done.10.refs_15_.refs_6_) | copy-start | bytes 3145732
  65.5 41.9 %copy-start.13 = (f32[256,1024]{1,0:T(8,128)}, f32[256,1024]{1,0:T(8,128)S(1)}, u32[]{:S(2)}) copy-start(f32[256,1024]{1,0:T(8,128)S(1)} %collective-permute-done.11.refs_17_.refs_8_) | copy-start | bytes 3145732
  65.5 41.9 %collective-permute-start.12 = (f32[256,1024]{1,0:T(8,128)S(1)}, f32[256,1024]{1,0:T(8,128)S(1)}, u32[]{:S(2)}, u32[]{:S(2)}) collective-permute-start(f32[256,1024]{1,0:T(8,128)S(1)} %collective-permute-done.10.refs_15_.refs_6_), channel_id=1, source_target_pairs={{24,0},{26,2},{28,4},{30,6},{0,8},{2,10},{4,12},{6,14},{8,16},{10,... | collective-permute-start | bytes 3145736 | tf_op jit(solution)/shard_map/ppermute | solution.py:298
  66.7 41.6 %collective-permute-start.13 = (f32[256,1024]{1,0:T(8,128)S(1)}, f32[256,1024]{1,0:T(8,128)S(1)}, u32[]{:S(2)}, u32[]{:S(2)}) collective-permute-start(f32[256,1024]{1,0:T(8,128)S(1)} %collective-permute-done.10.refs_15_.refs_6_), channel_id=1, source_target_pairs={{6,0},{0,2},{2,4},{4,6},{14,8},{8,10},{10,12},{12,14},{22,16},{16,... | collective-permute-start | bytes 3145736 | tf_op jit(solution)/shard_map/ppermute | solution.py:298
  102.0 34.0 %collective-permute-start.8 = (f32[256,1024]{1,0:T(8,128)}, f32[256,1024]{1,0:T(8,128)}, u32[]{:S(2)}, u32[]{:S(2)}) collective-permute-start(f32[256,1024]{1,0:T(8,128)} %copy-done.8), channel_id=1, source_target_pairs={{8,0},{10,2},{12,4},{14,6},{16,8},{18,10},{20,12},{22,14},{24,16},... | collective-permute-start | bytes 3145736 | tf_op jit(solution)/shard_map/ppermute | solution.py:298
  106.4 33.4 %collective-permute-start.4 = (f32[256,1024]{1,0:T(8,128)}, f32[256,1024]{1,0:T(8,128)}, u32[]{:S(2)}, u32[]{:S(2)}) collective-permute-start(f32[256,1024]{1,0:T(8,128)} %copy-done.7), channel_id=1, source_target_pairs={{2,0},{4,2},{6,4},{0,6},{10,8},{12,10},{14,12},{8,14},{18,16},{20,... | collective-permute-start | bytes 3145736 | tf_op jit(solution)/shard_map/ppermute | solution.py:298
  108.3 20.2 %collective-permute-start.14 = (f32[128,1024]{1,0:T(8,128)}, f32[128,1024]{1,0:T(8,128)}, u32[]{:S(2)}, u32[]{:S(2)}) collective-permute-start(f32[128,1024]{1,0:T(8,128)} %slice.16), channel_id=1, source_target_pairs={{6,0},{0,2},{2,4},{4,6},{14,8},{8,10},{10,12},{12,14},{22,16},{16,... | collective-permute-start | bytes 1572872 | tf_op jit(solution)/shard_map/ppermute | solution.py:298
  109.7 18.7 %collective-permute-start.15 = (f32[128,1024]{1,0:T(8,128)}, f32[128,1024]{1,0:T(8,128)}, u32[]{:S(2)}, u32[]{:S(2)}) collective-permute-start(f32[128,1024]{1,0:T(8,128)} %slice.17), channel_id=1, source_target_pairs={{24,0},{26,2},{28,4},{30,6},{0,8},{2,10},{4,12},{6,14},{8,16},{10,... | collective-permute-start | bytes 1572872 | tf_op jit(solution)/shard_map/ppermute | solution.py:298
  145.8 15.2 %collective-permute-start.16 = (f32[8,128,128]{2,1,0:T(8,128)}, f32[8,128,128]{2,1,0:T(8,128)S(1)}, u32[]{:S(2)}, u32[]{:S(2)}) collective-permute-start(f32[8,128,128]{2,1,0:T(8,128)} %get-tuple-element.41), channel_id=1, source_target_pairs={{0,1},{1,0},{2,3},{3,2},{4,5},{5,4},{6,7},{7,6},{8,9},{9,8},{10,11... | collective-permute-start | bytes 1572872 | tf_op jit(solution)/shard_map/ppermute | solution.py:302
  159.3 9.1 %collective-permute-start.17 = (f32[256,1024]{1,0:T(8,128)}, f32[256,1024]{1,0:T(8,128)S(1)}, u32[]{:S(2)}, u32[]{:S(2)}) collective-permute-start(f32[256,1024]{1,0:T(8,128)} %get-tuple-element.39.mine), channel_id=1, source_target_pairs={{0,1},{1,0},{2,3},{3,2},{4,5},{5,4},{6,7},{7,6},{8,9},{9,8},{10,11... | collective-permute-start | bytes 3145736 | tf_op jit(solution)/shard_map/ppermute | solution.py:302
  163.2 33.6 %all-to-all-start = ((f32[16,128,128]{2,1,0:T(8,128)}), f32[16,128,128]{2,1,0:T(8,128)S(1)}, u32[]{:S(2)}, u32[]{:S(2)}) async-start(f32[16,128,128]{2,1,0:T(8,128)} %pad_maximum_fusion.1), calls=%async_computation | async-start | bytes 2097152 | tf_op jit(solution)/shard_map/all_to_all | solution.py:307
  196.8 3.8 %collective-permute-start.18 = (f32[16,128,128]{2,1,0:T(8,128)S(1)}, f32[16,128,128]{2,1,0:T(8,128)S(1)}, u32[]{:S(2)}, u32[]{:S(2)}) collective-permute-start(f32[16,128,128]{2,1,0:T(8,128)S(1)} %all-to-all-done.mine), channel_id=1, source_target_pairs={{0,1},{1,0},{2,3},{3,2},{4,5},{5,4},{6,7},{7,6},{8,9},{9,8},{10,11... | collective-permute-start | bytes 3145736 | tf_op jit(solution)/shard_map/ppermute | solution.py:302
  212.7 2.5 collective-permute-start.19
  235.2 2.6 collective-permute-start.20
  264.1 4.5 %collective-permute-start.21 = (f32[16,192,128]{2,1,0:T(8,128)S(1)}, f32[16,192,128]{2,1,0:T(8,128)S(1)}, u32[]{:S(2)}, u32[]{:S(2)}) collective-permute-start(f32[16,192,128]{2,1,0:T(8,128)S(1)} %all_to_all.10.mine), channel_id=1, source_target_pairs={{0,1},{1,0},{2,3},{3,2},{4,5},{5,4},{6,7},{7,6},{8,9},{9,8},{10,11... | collective-permute-start | bytes 4718600 | tf_op jit(solution)/shard_map/ppermute | solution.py:302
  (17 other events, 132.0 us)
Sparse Core Ops, SparseCore 0:
  9.8 41.6 all-gather.2
  53.9 156.8 all-gather.4

commit v4 on v3

--- a/solution.py
+++ b/solution.py
@@ -195,8 +195,8 @@
             columns = slice(at, at + BLK)
             high[top:, columns], low[top:, columns] = split(jnp.where(ours, inners[q][...], inner_others[q][...]))
 
-    for n in range(0, lower.shape[1], TILE):
-        columns = slice(n, n + TILE)
+    for n in range(0, lower.shape[1], 2 * TILE):
+        columns = slice(n, n + 2 * TILE)
         total = three_pass(high, low, [lower.at[:, columns]], [lower.shape[0]])
 
         @pl.when(step == 0)
@@ -361,7 +361,7 @@
 
     halves = sum(HALVES, [])
     every_spots = chips(sum(PLACES, []))
-    late_spots = chips(PLACES[2]) * jnp.array([1, 1, 2, 2], jnp.int32) + jnp.array([0, 0, 0, 1], jnp.int32)
+    far_spots = chips(PLACES[2][2:]) * 2 + jnp.arange(2, dtype=jnp.int32)
 
     root_rows = lax.all_gather(root_inverse, ("leaf", "col"), axis=1, tiled=True)
 
@@ -372,8 +372,9 @@
     early = [own_upper, *near, *diagonal]
     cross, = cross_sum(None, root_rows, every_spots[:9], core_vector, early)
     fourth = fourth_round(near, third)
-    cross, = cross_sum(cross, root_rows, every_spots[9:13], core_vector, third)
-    cross, keep, give = cross_sum(cross, root_rows, late_spots, core_vector, fourth, True)
+    third_spots = jnp.concatenate([every_spots[9:13], far_spots])
+    cross, = cross_sum(cross, root_rows, third_spots, core_vector, [*third, *fourth[2:]])
+    cross, keep, give = cross_sum(cross, root_rows, every_spots[13:15], core_vector, fourth[:2], True)
     turned = turn(core, keep, give)
     picked = pick(blocks, core_vector, root_rows, cross, other_core(cross))
     turned = after(turned, *picked)

time: 287 us -> 285 us (level)
    unnamed x48 -> x40, local copies, waits for them, and re-layouts: 5.85 us -> 5.86 us
  transfers between devices with their start and end apart: 25 -> 25, of which waited for: 14 -> 15; matrix products, arithmetic and copies ran while one was open for 2% -> 2% of each run, Pallas kernels for 14% -> 14%
where the time goes in v4:
time: 285 us
  waiting for transfers between devices  124 us (44%)
  Pallas kernels  69.1 us (24%)
  starting transfers between devices  40.6 us (14%)
  blocking collectives  25 us (9%)
  between operations  14.2 us (5%)
  local copies, waits for them, and re-layouts  8.24 us (3%)
  other arithmetic  4.23 us (1%)
    ppermute x16, waiting for transfers between devices, pull(): return lax.ppermute(value, 'row', pairs)  90.5 us
    all_to_all x1, blocking collectives, turn(): return lax.all_to_all(sent, 'row', split_axis=0, concat_axis=0, tiled=True)  25 us
    pallas_call x3, Pallas kernels, cross_sum(): pl.pallas_call(functools.partial(cross_kernel, widths, base is not None,...  23.2 us
    all_to_all x1, waiting for transfers between devices, turn(): return lax.all_to_all(sent, 'row', split_axis=0, concat_axis=0, tiled=True)  21.5 us
    pallas_call x1, Pallas kernels, column_sum(): pl.pallas_call(column_kernel, grid_spec=pltpu.PrefetchScalarGridSpec(num_...  18.5 us
    ppermute x16, starting transfers between devices, pull(): return lax.ppermute(value, 'row', pairs)  17.8 us
    ppermute x6, starting transfers between devices, other_core(): return lax.ppermute(value, 'col', [(0, 1), (1, 0)])  17.7 us
    pallas_call x1, Pallas kernels, inner_sum(): pl.pallas_call(functools.partial(inner_kernel, pieces), grid_spec=pltpu.P...  11.1 us
  transfers between devices with their start and end apart: 25, of which 15 were waited for; matrix products, arithmetic and copies ran while one was open for 2% of the time, Pallas kernels for 14%

profile of v4, /device:TPU:225, one launch (start us, length us, event | category | flops | bytes accessed | tf_op | source)
XLA Modules:
  0.0 285.0 jit_solution(8689585166740658568)
XLA Ops:
  7.9 2.6 collective-permute-start
  10.5 2.7 collective-permute-start.1
  13.2 19.4 %collective-permute-done.refs_10_.refs_1_ = f32[256,1024]{1,0:T(8,128)S(1)} collective-permute-done((f32[256,1024]{1,0:T(8,128)}, f32[256,1024]{1,0:T(8,128)S(1)}, u32[]{:S(2)}, u32[]{:S(2)}) %collective-permute-start) | collective-permute-done | bytes 1048608 | tf_op jit(solution)/shard_map/ppermute | solution.py:298
  32.6 2.4 collective-permute-done.1.refs_12_.refs_3_
  35.1 3.1 %collective-permute-done.5.refs_11_.refs_2_ = f32[256,1024]{1,0:T(8,128)S(1)} collective-permute-done((f32[256,1024]{1,0:T(8,128)}, f32[256,1024]{1,0:T(8,128)S(1)}, u32[]{:S(2)}, u32[]{:S(2)}) %collective-permute-start.5) | collective-permute-done | bytes 1048608 | tf_op jit(solution)/shard_map/ppermute | solution.py:298
  38.2 2.5 collective-permute-start.2
  42.1 18.6 %collective-permute-done.2.refs_14_.refs_5_ = f32[256,1024]{1,0:T(8,128)S(1)} collective-permute-done((f32[256,1024]{1,0:T(8,128)S(1)}, f32[256,1024]{1,0:T(8,128)S(1)}, u32[]{:S(2)}, u32[]{:S(2)}) %collective-permute-start.2) | collective-permute-done | bytes 1048608 | tf_op jit(solution)/shard_map/ppermute | solution.py:298
  60.8 1.8 collective-permute-done.6.refs_16_.refs_7_
  63.6 1.5 collective-permute-start.7
  66.7 35.2 %collective-permute-done.7.refs_8_.refs_11_ = f32[256,1024]{1,0:T(8,128)S(1)} collective-permute-done((f32[256,1024]{1,0:T(8,128)S(1)}, f32[256,1024]{1,0:T(8,128)S(1)}, u32[]{:S(2)}, u32[]{:S(2)}) %collective-permute-start.7) | collective-permute-done | bytes 1048608 | tf_op jit(solution)/shard_map/ppermute | solution.py:298
  102.0 3.5 %collective-permute-start.8 = (f32[256,1024]{1,0:T(8,128)}, f32[256,1024]{1,0:T(8,128)}, u32[]{:S(2)}, u32[]{:S(2)}) collective-permute-start(f32[256,1024]{1,0:T(8,128)} %copy-done.8), channel_id=1, source_target_pairs={{8,0},{10,2},{12,4},{14,6},{16,8},{18,10},{20,12},{22,14},{24,16},... | collective-permute-start | bytes 3145736 | tf_op jit(solution)/shard_map/ppermute | solution.py:298
  111.5 11.1 %shard_map.137.refs_12_ = f32[256,1024]{1,0:T(8,128)} custom-call(s32[9]{0:T(128)} %bitcast.27, s32[1]{0:T(128)} %bitcast.core, f32[256,4096]{1,0:T(8,128)} %all-gather.3.cloned.1.call-done.refs_0_.refs_1_.refs_2_.refs_3_.refs_4_.refs_5_.refs_6_.refs_7_.refs_8_.root, ...), custom_call_target="tpu_custom_call" | custom-call | flops 1000 | bytes 1000 | tf_op jit(solution)/shard_map/pallas_call | solution.py:78
  122.6 3.8 %collective-permute-done.15.refs_11_.refs_16_ = f32[128,1024]{1,0:T(8,128)} collective-permute-done((f32[128,1024]{1,0:T(8,128)}, f32[128,1024]{1,0:T(8,128)}, u32[]{:S(2)}, u32[]{:S(2)}) %collective-permute-start.15) | collective-permute-done | bytes 524320 | tf_op jit(solution)/shard_map/ppermute | solution.py:298
  126.4 7.4 %shard_map.138.refs_4_ = f32[256,1024]{1,0:T(8,128)} custom-call(s32[6]{0:T(128)} %pad_add_fusion.spots, s32[1]{0:T(128)} %bitcast.core, f32[256,4096]{1,0:T(8,128)} %all-gather.3.cloned.1.call-done.refs_0_.refs_1_.refs_2_.refs_3_.refs_4_.refs_5_.refs_6_.refs_7_.refs_8_.root, ...), custom_call_target="tpu_custom_call" | custom-call | flops 1000 | bytes 1000 | tf_op jit(solution)/shard_map/pallas_call | solution.py:78
  133.8 2.2 collective-permute-done.8.refs_3_.refs_14_
  136.0 3.8 %collective-permute-done.4.refs_2_.refs_13_ = f32[256,1024]{1,0:T(8,128)} collective-permute-done((f32[256,1024]{1,0:T(8,128)}, f32[256,1024]{1,0:T(8,128)}, u32[]{:S(2)}, u32[]{:S(2)}) %collective-permute-start.4) | collective-permute-done | bytes 1048608 | tf_op jit(solution)/shard_map/ppermute | solution.py:298
  139.9 4.7 %shard_map.139 = (f32[256,1024]{1,0:T(8,128)}, f32[8,128,128]{2,1,0:T(8,128)}, f32[8,128,128]{2,1,0:T(8,128)}) custom-call(s32[2]{0:T(128)} %slice.15.spots, s32[1]{0:T(128)} %bitcast.core, f32[256,4096]{1,0:T(8,128)} %all-gather.3.cloned.1.call-done.refs_0_.refs_1_.refs_2_.refs_3_.refs_4_.refs_5_.refs_6_.refs_7_.refs_8_.root, ...), custom_call_target="tpu_custom_call" | custom-call | flops 1000 | bytes 1000 | tf_op jit(solution)/shard_map/pallas_call | solution.py:78
  144.6 13.5 %collective-permute-start.16 = (f32[8,128,128]{2,1,0:T(8,128)}, f32[8,128,128]{2,1,0:T(8,128)S(1)}, u32[]{:S(2)}, u32[]{:S(2)}) collective-permute-start(f32[8,128,128]{2,1,0:T(8,128)} %get-tuple-element.41), channel_id=1, source_target_pairs={{0,1},{1,0},{2,3},{3,2},{4,5},{5,4},{6,7},{7,6},{8,9},{9,8},{10,11... | collective-permute-start | bytes 1572872 | tf_op jit(solution)/shard_map/ppermute | solution.py:302
  158.2 1.7 collective-permute-done.16
  162.0 5.1 %all-to-all-start = ((f32[16,128,128]{2,1,0:T(8,128)}), f32[16,128,128]{2,1,0:T(8,128)S(1)}, u32[]{:S(2)}, u32[]{:S(2)}) async-start(f32[16,128,128]{2,1,0:T(8,128)} %pad_maximum_fusion.1), calls=%async_computation | async-start | bytes 2097152 | tf_op jit(solution)/shard_map/all_to_all | solution.py:307
  168.1 6.0 %shard_map.140 = (bf16[256,4096]{1,0:T(8,128)(2,1)}, bf16[256,4096]{1,0:T(8,128)(2,1)}) custom-call(s32[16]{0:T(128)} %bitcast.24, s32[1]{0:T(128)} %bitcast.core, f32[256,4096]{1,0:T(8,128)} %all-gather.3.cloned.1.call-done.refs_0_.refs_1_.refs_2_.refs_3_.refs_4_.refs_5_.refs_6_.refs_7_.refs_8_.root, f32[256,1024]{1,0:T(8,128)} %get-tuple-element.39.mine, ...), custom_call_target="tpu_custom_call" | custom-call | bytes 20971520 | tf_op jit(solution)/shard_map/pallas_call | solution.py:160
  174.1 21.5 %all-to-all-done.mine = f32[16,128,128]{2,1,0:T(8,128)S(1)} async-done(((f32[16,128,128]{2,1,0:T(8,128)}), f32[16,128,128]{2,1,0:T(8,128)S(1)}, u32[]{:S(2)}, u32[]{:S(2)}) %all-to-all-start) | async-done | bytes 1048608 | tf_op jit(solution)/shard_map/all_to_all | solution.py:307
  195.6 1.5 collective-permute-start.18
  197.1 2.3 collective-permute-done.18.theirs
  200.4 11.1 %shard_map.141 = (f32[128,1024]{1,0:T(8,128)}, bf16[128,4096]{1,0:T(8,128)(2,1)}, bf16[128,4096]{1,0:T(8,128)(2,1)}) custom-call(s32[17]{0:T(128)} %copy-done.17, s32[1]{0:T(128)} %bitcast.core, f32[16,128,128]{2,1,0:T(8,128)} %copy-done.6, f32[16,128,128]{2,1,0:T(8,128)} %copy-done.15, f32[256,1024]{1,0:T(8,128)} %bitcast.18, f32[256,1024]{1,0:T(8,128)} %copy-done.7, ...), custom_call_target="tpu_custom_call" | custom-call | flops 1000 | bytes 1000 | tf_op jit(solution)/shard_map/pallas_call | solution.py:122
  212.2 1.8 collective-permute-done.19.refs_12_.refs_13_.refs_14_.refs_15_
  214.8 18.5 %shard_map.142 = (f32[256,1024]{1,0:T(8,128)}, f32[128,1024]{1,0:T(8,128)}, f32[8,192,128]{2,1,0:T(8,128)}, f32[8,192,128]{2,1,0:T(8,128)}) custom-call(s32[16]{0:T(128)} %bitcast.25, s32[1]{0:T(128)} %bitcast.core, bf16[256,4096]{1,0:T(8,128)(2,1)} %get-tuple-element.42.top_high, bf16[256,4096]{1,0:T(8,128)(2,1)} %get-tuple-element.43.top_low, ...), custom_call_target="tpu_custom_call" | custom-call | flops 1000 | bytes 1000 | tf_op jit(solution)/shard_map/pallas_call | solution.py:235
  233.8 2.1 collective-permute-done.20
  237.3 25.0 %all_to_all.10.mine = f32[16,192,128]{2,1,0:T(8,128)S(1)} all-to-all(f32[16,192,128]{2,1,0:T(8,128)S(1)} %pad_maximum_fusion), channel_id=1, replica_groups=mesh['leaf'=8,'row'=16,'col'=2] {'row'}, dimensions={0} | all-to-all | bytes 3145728 | tf_op jit(solution)/shard_map/all_to_all | solution.py:307
  262.3 1.5 collective-permute-start.21
  263.8 3.0 %collective-permute-done.21.theirs = f32[16,192,128]{2,1,0:T(8,128)S(1)} collective-permute-done((f32[16,192,128]{2,1,0:T(8,128)S(1)}, f32[16,192,128]{2,1,0:T(8,128)S(1)}, u32[]{:S(2)}, u32[]{:S(2)}) %collective-permute-start.21) | collective-permute-done | bytes 1572896 | tf_op jit(solution)/shard_map/ppermute | solution.py:302
  267.9 10.2 %shard_map.143 = f32[128,1024]{1,0:T(8,128)} custom-call(s32[16]{0:T(128)} %bitcast.26, s32[1]{0:T(128)} %bitcast.core, f32[16,192,128]{2,1,0:T(8,128)} %copy-done.3, f32[16,192,128]{2,1,0:T(8,128)} %copy-done.14, f32[4096,1024]{1,0:T(8,128)} %all-gather.5.cloned.1.call-done.refs_16_.lower, f32[128,1024]{1,0:T(8,128)} %bitcast.22), custom_call_target="tpu_custom_call" | custom-call | flops 1000 | bytes 1000 | tf_op jit(solution)/shard_map/pallas_call | solution.py:274
  (79 shorter events, 19.5 us)
Async XLA Ops:
  7.2 104.3 %all-gather.3.cloned.1.call-start = ((), (), s32[]{:S(2)}) async-start(), calls=%async_computation.2 | async-start | bytes 4456448 | tf_op jit(solution)/shard_map/all_gather | solution.py:366
  7.9 206.1 %all-gather.5.cloned.1.call-start = ((), (), s32[]{:S(2)}) async-start(), calls=%async_computation.3 | async-start | bytes 17825792 | tf_op jit(solution)/shard_map/all_gather | solution.py:371
  7.9 24.7 %collective-permute-start = (f32[256,1024]{1,0:T(8,128)}, f32[256,1024]{1,0:T(8,128)S(1)}, u32[]{:S(2)}, u32[]{:S(2)}) collective-permute-start(f32[256,1024]{1,0:T(8,128)} %bitcast.13), channel_id=1, source_target_pairs={{2,0},{4,2},{6,4},{0,6},{10,8},{12,10},{14,12},{8,14},{18,16},{20,... | collective-permute-start | bytes 3145736 | tf_op jit(solution)/shard_map/ppermute | solution.py:298
  10.5 24.6 %collective-permute-start.1 = (f32[256,1024]{1,0:T(8,128)}, f32[256,1024]{1,0:T(8,128)S(1)}, u32[]{:S(2)}, u32[]{:S(2)}) collective-permute-start(f32[256,1024]{1,0:T(8,128)} %bitcast.14), channel_id=1, source_target_pairs={{8,0},{10,2},{12,4},{14,6},{16,8},{18,10},{20,12},{22,14},{24,16},... | collective-permute-start | bytes 3145736 | tf_op jit(solution)/shard_map/ppermute | solution.py:298
  13.2 24.9 %collective-permute-start.5 = (f32[256,1024]{1,0:T(8,128)}, f32[256,1024]{1,0:T(8,128)S(1)}, u32[]{:S(2)}, u32[]{:S(2)}) collective-permute-start(f32[256,1024]{1,0:T(8,128)} %bitcast.15), channel_id=1, source_target_pairs={{6,0},{0,2},{2,4},{4,6},{14,8},{8,10},{10,12},{12,14},{22,16},{16,... | collective-permute-start | bytes 3145736 | tf_op jit(solution)/shard_map/ppermute | solution.py:298
  13.2 24.9 %collective-permute-start.9 = (f32[256,1024]{1,0:T(8,128)}, f32[256,1024]{1,0:T(8,128)}, u32[]{:S(2)}, u32[]{:S(2)}) collective-permute-start(f32[256,1024]{1,0:T(8,128)} %bitcast.16), channel_id=1, source_target_pairs={{24,0},{26,2},{28,4},{30,6},{0,8},{2,10},{4,12},{6,14},{8,16},{10,... | collective-permute-start | bytes 3145736 | tf_op jit(solution)/shard_map/ppermute | solution.py:298
  32.6 32.8 %copy-start.7 = (f32[256,1024]{1,0:T(8,128)}, f32[256,1024]{1,0:T(8,128)S(1)}, u32[]{:S(2)}) copy-start(f32[256,1024]{1,0:T(8,128)S(1)} %collective-permute-done.refs_10_.refs_1_) | copy-start | bytes 3145732
  38.2 27.3 %copy-start.9 = (f32[256,1024]{1,0:T(8,128)}, f32[256,1024]{1,0:T(8,128)S(1)}, u32[]{:S(2)}) copy-start(f32[256,1024]{1,0:T(8,128)S(1)} %collective-permute-done.5.refs_11_.refs_2_) | copy-start | bytes 3145732
  38.2 72.0 %copy-start.18 = (s32[17]{0:T(128)S(1)}, s32[17]{0:T(128)}, u32[]{:S(2)}) copy-start(s32[17]{0:T(128)} %constant.74.clone) | copy-start | bytes 208
  38.2 72.0 %copy-start.19 = (s32[17]{0:T(128)S(1)}, s32[17]{0:T(128)}, u32[]{:S(2)}) copy-start(s32[17]{0:T(128)} %constant.75.clone) | copy-start | bytes 208
  38.2 22.6 %collective-permute-start.2 = (f32[256,1024]{1,0:T(8,128)S(1)}, f32[256,1024]{1,0:T(8,128)S(1)}, u32[]{:S(2)}, u32[]{:S(2)}) collective-permute-start(f32[256,1024]{1,0:T(8,128)S(1)} %collective-permute-done.1.refs_12_.refs_3_), channel_id=1, source_target_pairs={{2,0},{4,2},{6,4},{0,6},{10,8},{12,10},{14,12},{8,14},{18,16},{20,... | collective-permute-start | bytes 3145736 | tf_op jit(solution)/shard_map/ppermute | solution.py:298
  40.7 21.9 %collective-permute-start.6 = (f32[256,1024]{1,0:T(8,128)S(1)}, f32[256,1024]{1,0:T(8,128)S(1)}, u32[]{:S(2)}, u32[]{:S(2)}) collective-permute-start(f32[256,1024]{1,0:T(8,128)S(1)} %collective-permute-done.5.refs_11_.refs_2_), channel_id=1, source_target_pairs={{8,0},{10,2},{12,4},{14,6},{16,8},{18,10},{20,12},{22,14},{24,16},... | collective-permute-start | bytes 3145736 | tf_op jit(solution)/shard_map/ppermute | solution.py:298
  40.7 24.8 %collective-permute-start.10 = (f32[256,1024]{1,0:T(8,128)}, f32[256,1024]{1,0:T(8,128)S(1)}, u32[]{:S(2)}, u32[]{:S(2)}) collective-permute-start(f32[256,1024]{1,0:T(8,128)} %collective-permute-done.9.refs_13_.refs_4_), channel_id=1, source_target_pairs={{6,0},{0,2},{2,4},{4,6},{14,8},{8,10},{10,12},{12,14},{22,16},{16,... | collective-permute-start | bytes 3145736 | tf_op jit(solution)/shard_map/ppermute | solution.py:298
  40.7 24.8 %collective-permute-start.12 = (f32[256,1024]{1,0:T(8,128)S(1)}, f32[256,1024]{1,0:T(8,128)S(1)}, u32[]{:S(2)}, u32[]{:S(2)}) collective-permute-start(f32[256,1024]{1,0:T(8,128)S(1)} %collective-permute-done.refs_10_.refs_1_), channel_id=1, source_target_pairs={{24,0},{26,2},{28,4},{30,6},{0,8},{2,10},{4,12},{6,14},{8,16},{10,... | collective-permute-start | bytes 3145736 | tf_op jit(solution)/shard_map/ppermute | solution.py:298
  60.8 46.6 %copy-start.10 = (f32[256,1024]{1,0:T(8,128)}, f32[256,1024]{1,0:T(8,128)S(1)}, u32[]{:S(2)}) copy-start(f32[256,1024]{1,0:T(8,128)S(1)} %collective-permute-done.2.refs_14_.refs_5_) | copy-start | bytes 3145732
  63.6 38.4 %collective-permute-start.7 = (f32[256,1024]{1,0:T(8,128)S(1)}, f32[256,1024]{1,0:T(8,128)S(1)}, u32[]{:S(2)}, u32[]{:S(2)}) collective-permute-start(f32[256,1024]{1,0:T(8,128)S(1)} %collective-permute-done.2.refs_14_.refs_5_), channel_id=1, source_target_pairs={{8,0},{10,2},{12,4},{14,6},{16,8},{18,10},{20,12},{22,14},{24,16},... | collective-permute-start | bytes 3145736 | tf_op jit(solution)/shard_map/ppermute | solution.py:298
  65.1 40.4 %collective-permute-start.3 = (f32[256,1024]{1,0:T(8,128)S(1)}, f32[256,1024]{1,0:T(8,128)S(1)}, u32[]{:S(2)}, u32[]{:S(2)}) collective-permute-start(f32[256,1024]{1,0:T(8,128)S(1)} %collective-permute-done.2.refs_14_.refs_5_), channel_id=1, source_target_pairs={{2,0},{4,2},{6,4},{0,6},{10,8},{12,10},{14,12},{8,14},{18,16},{20,... | collective-permute-start | bytes 3145736 | tf_op jit(solution)/shard_map/ppermute | solution.py:298
  65.5 42.8 %copy-start.12 = (f32[256,1024]{1,0:T(8,128)}, f32[256,1024]{1,0:T(8,128)S(1)}, u32[]{:S(2)}) copy-start(f32[256,1024]{1,0:T(8,128)S(1)} %collective-permute-done.10.refs_15_.refs_6_) | copy-start | bytes 3145732
  65.5 41.9 %copy-start.13 = (f32[256,1024]{1,0:T(8,128)}, f32[256,1024]{1,0:T(8,128)S(1)}, u32[]{:S(2)}) copy-start(f32[256,1024]{1,0:T(8,128)S(1)} %collective-permute-done.12.refs_17_.refs_8_) | copy-start | bytes 3145732
  65.5 41.9 %collective-permute-start.13 = (f32[256,1024]{1,0:T(8,128)S(1)}, f32[256,1024]{1,0:T(8,128)S(1)}, u32[]{:S(2)}, u32[]{:S(2)}) collective-permute-start(f32[256,1024]{1,0:T(8,128)S(1)} %collective-permute-done.10.refs_15_.refs_6_), channel_id=1, source_target_pairs={{24,0},{26,2},{28,4},{30,6},{0,8},{2,10},{4,12},{6,14},{8,16},{10,... | collective-permute-start | bytes 3145736 | tf_op jit(solution)/shard_map/ppermute | solution.py:298
  66.7 41.6 %collective-permute-start.11 = (f32[256,1024]{1,0:T(8,128)S(1)}, f32[256,1024]{1,0:T(8,128)S(1)}, u32[]{:S(2)}, u32[]{:S(2)}) collective-permute-start(f32[256,1024]{1,0:T(8,128)S(1)} %collective-permute-done.10.refs_15_.refs_6_), channel_id=1, source_target_pairs={{6,0},{0,2},{2,4},{4,6},{14,8},{8,10},{10,12},{12,14},{22,16},{16,... | collective-permute-start | bytes 3145736 | tf_op jit(solution)/shard_map/ppermute | solution.py:298
  102.0 34.0 %collective-permute-start.8 = (f32[256,1024]{1,0:T(8,128)}, f32[256,1024]{1,0:T(8,128)}, u32[]{:S(2)}, u32[]{:S(2)}) collective-permute-start(f32[256,1024]{1,0:T(8,128)} %copy-done.8), channel_id=1, source_target_pairs={{8,0},{10,2},{12,4},{14,6},{16,8},{18,10},{20,12},{22,14},{24,16},... | collective-permute-start | bytes 3145736 | tf_op jit(solution)/shard_map/ppermute | solution.py:298
  106.4 33.4 %collective-permute-start.4 = (f32[256,1024]{1,0:T(8,128)}, f32[256,1024]{1,0:T(8,128)}, u32[]{:S(2)}, u32[]{:S(2)}) collective-permute-start(f32[256,1024]{1,0:T(8,128)} %copy-done.7), channel_id=1, source_target_pairs={{2,0},{4,2},{6,4},{0,6},{10,8},{12,10},{14,12},{8,14},{18,16},{20,... | collective-permute-start | bytes 3145736 | tf_op jit(solution)/shard_map/ppermute | solution.py:298
  108.3 14.3 %collective-permute-start.14 = (f32[128,1024]{1,0:T(8,128)}, f32[128,1024]{1,0:T(8,128)}, u32[]{:S(2)}, u32[]{:S(2)}) collective-permute-start(f32[128,1024]{1,0:T(8,128)} %slice.20), channel_id=1, source_target_pairs={{6,0},{0,2},{2,4},{4,6},{14,8},{8,10},{10,12},{12,14},{22,16},{16,... | collective-permute-start | bytes 1572872 | tf_op jit(solution)/shard_map/ppermute | solution.py:298
  109.7 16.7 %collective-permute-start.15 = (f32[128,1024]{1,0:T(8,128)}, f32[128,1024]{1,0:T(8,128)}, u32[]{:S(2)}, u32[]{:S(2)}) collective-permute-start(f32[128,1024]{1,0:T(8,128)} %slice.21), channel_id=1, source_target_pairs={{24,0},{26,2},{28,4},{30,6},{0,8},{2,10},{4,12},{6,14},{8,16},{10,... | collective-permute-start | bytes 1572872 | tf_op jit(solution)/shard_map/ppermute | solution.py:298
  144.6 15.3 %collective-permute-start.16 = (f32[8,128,128]{2,1,0:T(8,128)}, f32[8,128,128]{2,1,0:T(8,128)S(1)}, u32[]{:S(2)}, u32[]{:S(2)}) collective-permute-start(f32[8,128,128]{2,1,0:T(8,128)} %get-tuple-element.41), channel_id=1, source_target_pairs={{0,1},{1,0},{2,3},{3,2},{4,5},{5,4},{6,7},{7,6},{8,9},{9,8},{10,11... | collective-permute-start | bytes 1572872 | tf_op jit(solution)/shard_map/ppermute | solution.py:302
  158.1 9.1 %collective-permute-start.17 = (f32[256,1024]{1,0:T(8,128)}, f32[256,1024]{1,0:T(8,128)S(1)}, u32[]{:S(2)}, u32[]{:S(2)}) collective-permute-start(f32[256,1024]{1,0:T(8,128)} %get-tuple-element.39.mine), channel_id=1, source_target_pairs={{0,1},{1,0},{2,3},{3,2},{4,5},{5,4},{6,7},{7,6},{8,9},{9,8},{10,11... | collective-permute-start | bytes 3145736 | tf_op jit(solution)/shard_map/ppermute | solution.py:302
  162.0 33.6 %all-to-all-start = ((f32[16,128,128]{2,1,0:T(8,128)}), f32[16,128,128]{2,1,0:T(8,128)S(1)}, u32[]{:S(2)}, u32[]{:S(2)}) async-start(f32[16,128,128]{2,1,0:T(8,128)} %pad_maximum_fusion.1), calls=%async_computation | async-start | bytes 2097152 | tf_op jit(solution)/shard_map/all_to_all | solution.py:307
  195.6 3.8 %collective-permute-start.18 = (f32[16,128,128]{2,1,0:T(8,128)S(1)}, f32[16,128,128]{2,1,0:T(8,128)S(1)}, u32[]{:S(2)}, u32[]{:S(2)}) collective-permute-start(f32[16,128,128]{2,1,0:T(8,128)S(1)} %all-to-all-done.mine), channel_id=1, source_target_pairs={{0,1},{1,0},{2,3},{3,2},{4,5},{5,4},{6,7},{7,6},{8,9},{9,8},{10,11... | collective-permute-start | bytes 3145736 | tf_op jit(solution)/shard_map/ppermute | solution.py:302
  211.6 2.4 collective-permute-start.19
  233.3 2.6 collective-permute-start.20
  262.3 4.5 %collective-permute-start.21 = (f32[16,192,128]{2,1,0:T(8,128)S(1)}, f32[16,192,128]{2,1,0:T(8,128)S(1)}, u32[]{:S(2)}, u32[]{:S(2)}) collective-permute-start(f32[16,192,128]{2,1,0:T(8,128)S(1)} %all_to_all.10.mine), channel_id=1, source_target_pairs={{0,1},{1,0},{2,3},{3,2},{4,5},{5,4},{6,7},{7,6},{8,9},{9,8},{10,11... | collective-permute-start | bytes 4718600 | tf_op jit(solution)/shard_map/ppermute | solution.py:302
  (13 other events, 91.1 us)
Sparse Core Ops, SparseCore 0:
  9.8 41.6 all-gather.2
  53.9 156.9 all-gather.4
